TPU v7x, 512 devices: a whole 4x8x8 slice. The times are simulated.
512 devices in a mesh: grp: 16 (over z, y_hi), head: 32 (over y_lo, x, core).
Axes of the slice: x: 4, y: 8 (y_hi: 2, y_lo: 4; y = y_hi * 4 + y_lo), z: 8, core: 2. Of those that a mesh axis runs over, the one named last changes fastest.
Arguments:
- cache: bfloat16 [512, 2, 8, 128, 128], P(('grp', 'head')), parts along dimension 0, may hold values from -6 to 6
- fresh: bfloat16 [512, 3, 2, 8, 128], P(('grp', 'head')), parts along dimension 0, may hold values from -6 to 6
- slot_map: int32 [1024], P('grp'), parts along dimension 0, may hold values from 0 to 7, as said below
- lengths: int32 [64], P('grp'), parts along dimension 0, may hold values from 1 to 128, 256 in all
- out_weight: bfloat16 [8192, 6144], P('head'), may hold values from -1.5 to 1.5
- residual: bfloat16 [64, 2, 6144], P('grp', None, 'head'), parts along dimension 0, may hold values from -6 to 6
- norm_gain: float32 [6144], replicated, may hold values from 0.25 to 1.75
- norm_bias: float32 [6144], replicated, may hold values from -3 to 3
Outputs:
- cache_new: bfloat16 [512, 4, 2, 2, 128, 128], P(('grp', 'head')), parts along dimension 0
- hidden: bfloat16 [64, 2, 6144], P('grp', None, 'head'), parts along dimension 0
- normed: bfloat16 [64, 2, 6144], P('grp'), parts along dimension 0
There are 16 independent parts, one for each index of `grp`. A program takes and returns all parts, laid end to end along the dimension named above; an argument that names none is the same for every part. Nothing has to cross between parts.
Inputs may be any that keep to these rules, and one draw needn't show every extreme that they name: `slot_map`: for each old member m, the entries of the new members r * 8 + m (r below 4) together take each of its 8 slots once.
All inputs are finite; a program needn't handle non-finite values.
Results may differ from a plain program's by a relative error of at most 0.0061.
Values may be sent and summed in bfloat16 or wider, within the bound.
No kernel may reach another device: no remote copies, remote signals or barrier semaphores. Data moves between devices by JAX's collectives and lax.ppermute only.
A program may use at most 64 MiB of HBM per device.

v0:
```python
import math

import jax
import jax.numpy as jnp
from jax import lax
from jax.sharding import PartitionSpec as P

ROWS = 4
HEAD_DEV = 2
HEAD_DIM = 128
OUT = 6144


def shifted(shard, axis, by):
    length = lax.axis_size(axis)
    return lax.ppermute(shard, axis, [(i, (i + by) % length) for i in range(length)])


def attend(kv_block, fresh_block, lens):
    keys = kv_block[:, 0]
    vals = kv_block[:, 1]
    query = fresh_block[:, 0]
    new_keys = fresh_block[:, 1]
    new_vals = fresh_block[:, 2]
    scale = 1.0 / math.sqrt(keys.shape[-1])
    positions = jnp.arange(keys.shape[2], dtype=jnp.int32)
    visible = positions[None, None, :] < lens[:, None, None]
    upto = jnp.arange(2)[None, None, :]
    results = []
    for step in range(2):
        single = query[:, step]
        old_scores = (
            jnp.einsum("bhd,bhpd->bhp", single, keys, preferred_element_type=jnp.float32) * scale
        )
        old_scores = jnp.where(visible, old_scores, -1e30)
        new_scores = (
            jnp.einsum("bhd,buhd->bhu", single, new_keys, preferred_element_type=jnp.float32)
            * scale
        )
        new_scores = jnp.where(upto <= step, new_scores, -1e30)
        top = jnp.maximum(old_scores.max(-1), new_scores.max(-1))[..., None]
        old_exp = jnp.where(visible, jnp.exp(old_scores - top), 0.0)
        new_exp = jnp.where(upto <= step, jnp.exp(new_scores - top), 0.0)
        total = old_exp.sum(-1, keepdims=True) + new_exp.sum(-1, keepdims=True)
        old_w = (old_exp / total).astype(jnp.bfloat16)
        new_w = (new_exp / total).astype(jnp.bfloat16)
        result = jnp.einsum("bhp,bhpd->bhd", old_w, vals, preferred_element_type=jnp.float32)
        result = result + jnp.einsum(
            "bhu,buhd->bhd", new_w, new_vals, preferred_element_type=jnp.float32
        )
        results.append(result)
    return jnp.stack(results, axis=1)


def select_heads(cache, extra, extra_axis, slot_map, target):
    wanted = lax.dynamic_slice_in_dim(slot_map, target * HEAD_DEV, HEAD_DEV)
    return (jnp.take(cache[0], wanted, axis=1), jnp.take(extra, wanted, axis=extra_axis))


def move_heads(cache, extra, extra_axis, slot_map):
    members = lax.axis_size("head")
    old_count = members // ROWS
    me = lax.axis_index("head")
    my_row = me // old_count
    kv_list = []
    extra_list = []
    for offset in range(ROWS):
        target = (me + offset * old_count) % members
        kv_part, extra_part = select_heads(cache, extra, extra_axis, slot_map, target)
        if offset > 0:
            kv_part, extra_part = shifted((kv_part, extra_part), "head", offset * old_count)
        kv_list.append(kv_part)
        extra_list.append(extra_part)
    source_rows = (my_row - jnp.arange(ROWS, dtype=jnp.int32)) % ROWS
    kv_rows = jnp.take(jnp.stack(kv_list), source_rows, axis=0)
    extra_rows = jnp.take(jnp.stack(extra_list), source_rows, axis=0)
    return (kv_rows, extra_rows)


def normalize(values, mean, var, gain, bias):
    return ((values - mean) / jnp.sqrt(var + 1e-05) * gain + bias).astype(jnp.bfloat16)


def body(cache, fresh, slot_map, lengths, out_weight, residual, norm_gain, norm_bias):
    me = lax.axis_index("head")
    kv_rows, fresh_rows = move_heads(cache, fresh[0], 2, slot_map)
    attended = attend(kv_rows, fresh_rows, lengths).astype(jnp.bfloat16)
    cache_new = kv_rows[None]
    features = attended.reshape(ROWS * 2, HEAD_DEV * HEAD_DIM)
    partial_value = jnp.dot(features, out_weight, preferred_element_type=jnp.float32)
    share = residual.shape[-1]
    own_residual = residual.reshape(ROWS * 2, share).astype(jnp.float32)
    summed = lax.psum_scatter(partial_value, "head", scatter_dimension=1, tiled=True)
    hidden = (own_residual + summed).astype(jnp.bfloat16)
    values = hidden.astype(jnp.float32)
    total = lax.psum(jnp.sum(values, axis=-1), "head")
    mean = (total / OUT)[..., None]
    spread = lax.psum(jnp.sum((values - mean) ** 2, axis=-1), "head")
    var = (spread / OUT)[..., None]
    gain_part = lax.dynamic_slice_in_dim(norm_gain, me * share, share)
    bias_part = lax.dynamic_slice_in_dim(norm_bias, me * share, share)
    normed_part = normalize(values, mean, var, gain_part, bias_part)
    normed_full = lax.all_gather(normed_part, "head", axis=1, tiled=True)
    return (cache_new, hidden.reshape(ROWS, 2, share), normed_full.reshape(ROWS, 2, OUT))


def solution(mesh):
    in_specs = (
        P(("grp", "head"), None, None, None, None),
        P(("grp", "head"), None, None, None, None),
        P("grp"),
        P("grp"),
        P("head", None),
        P("grp", None, "head"),
        P(),
        P(),
    )
    out_specs = (
        P(("grp", "head"), None, None, None, None, None),
        P("grp", None, "head"),
        P("grp", None, None),
    )
    return jax.shard_map(body, mesh=mesh, in_specs=in_specs, out_specs=out_specs, check_vma=False)
```

profile of v0, /device:TPU:1, one launch (start us, length us, event | category | flops | bytes accessed | tf_op | source)
XLA Modules:
  0.0 410.8 jit_solution(14563503728136553850)
XLA Ops:
  7.3 1.5 compare_and_fusion.3
  8.8 1.6 gather_fusion.3
  10.5 4.0 collective-permute-start
  14.5 1.6 gather_fusion.4
  16.2 0.7 select_bitcast_fusion.1
  16.9 4.2 %collective-permute-start.1 = (bf16[2,2,128,128]{3,2,0,1:T(8,128)(2,1)}, bf16[2,2,128,128]{3,2,0,1:T(8,128)(2,1)}, u32[]{:S(2)}, u32[]{:S(2)}) collective-permute-start(bf16[2,2,128,128]{3,2,0,1:T(8,128)(2,1)} %select_bitcast_fusion.1), channel_id=1, source_target_pairs={{0,16},{1,17},{2,18},{3,19},{4,20},{5,21},{6,22},{7,23},{8,24},{9,... | collective-permute-start | bytes 393224 | tf_op jit(solution)/shard_map/ppermute | solution.py:16
  21.1 0.7 copy.62
  21.8 0.6 gather_fusion.7
  22.4 0.7 fusion.18
  23.1 1.9 collective-permute-start.3
  25.0 0.6 gather_fusion.8
  25.6 0.7 fusion.19
  26.2 3.2 collective-permute-start.4
  29.5 0.6 gather_fusion.9
  30.1 0.7 fusion.20
  30.7 3.8 collective-permute-start.5
  34.6 1.6 gather_fusion.5
  36.2 0.5 fusion.39
  36.7 0.5 compare_and_fusion.4
  37.3 0.6 copy-done.4
  37.9 1.6 gather_fusion.2
  39.5 0.7 gather_fusion.6
  40.2 0.6 iota_compare_fusion.1
  40.8 1.4 select_bitcast_fusion
  42.2 1.2 pad_clamp_fusion
  43.4 0.7 select_bitcast_fusion.3
  44.1 0.7 fusion.17
  44.8 1.3 iota_compare_fusion
  46.2 0.5 iota_compare_fusion.2
  46.7 2.2 collective-permute-start.2
  48.9 0.7 pad_maximum_fusion.1
  49.6 1.3 gather_fusion.1
  50.9 0.8 broadcast_select_fusion.1
  51.9 0.5 copy-done.10
  52.3 0.7 fusion.24
  53.0 0.7 copy.24
  53.7 0.8 copy.31
  54.5 1.4 fusion.40
  55.9 1.0 pad_maximum_fusion
  56.9 0.8 copy.19
  57.8 2.6 gather_fusion
  60.3 1.2 broadcast_select_fusion
  61.5 0.2 fusion.1
  61.7 0.6 copy-done.1
  62.3 0.2 fusion
  62.8 0.1 fusion.21
  63.1 0.2 fusion.31
  63.3 0.1 fusion.26
  63.5 1.1 fusion.3
  65.0 1.1 fusion.2
  66.1 3.0 convolution_bitcast_fusion
  69.2 0.7 copy-done.7
  69.9 0.8 dynamic_slice.22
  70.6 0.8 dynamic_slice.23
  71.4 1.9 bitcast_select_fusion
  73.4 148.8 %reduce-scatter.4.cloned.1.call-done = f32[192,8]{1,0:T(8,128)} async-done(((f32[6144,8]{1,0:T(8,128)}), f32[192,8]{1,0:T(8,128)}) %reduce-scatter.4.cloned.1.call-update) | async-done | bytes 6160
  222.1 0.9 copy.37
  223.2 71.8 %psum.14 = f32[8]{0:T(128)S(1)} all-reduce(f32[8]{0:T(128)S(1)} %get-tuple-element.7), channel_id=1, replica_groups=mesh['grp'=16,'head'=32] {'head'}, use_global_device_ids=true, to_apply=%region_10.13 | all-reduce | flops 8 | bytes 64 | tf_op jit(solution)/shard_map/psum | solution.py:96
  295.0 0.2 fusion.6
  295.2 0.6 reshape.148
  295.8 68.7 %psum.15 = f32[8]{0:T(128)S(1)} all-reduce(f32[8]{0:T(128)S(1)} %fusion.6), channel_id=1, replica_groups=mesh['grp'=16,'head'=32] {'head'}, use_global_device_ids=true, to_apply=%region_12.15 | all-reduce | flops 8 | bytes 64 | tf_op jit(solution)/shard_map/psum | solution.py:98
  364.6 38.4 %all-gather = bf16[32,192,8]{1,2,0:T(8,128)(2,1)S(1)} all-gather(bf16[1,192,8]{1,2,0:T(8,128)(2,1)S(1)} %fusion.10), channel_id=1, replica_groups=mesh['grp'=16,'head'=32] {'head'}, dimensions={0}, use_global_device_ids=true | all-gather | bytes 101376 | tf_op jit(solution)/shard_map/all_gather | solution.py:103
  403.0 0.2 reshape.240
  403.2 0.7 reshape.149
  (61 shorter events, 1.4 us)
Async XLA Ops:
  7.2 59.0 %copy-start = (bf16[256,6144]{1,0:T(8,128)(2,1)S(1)}, bf16[256,6144]{1,0:T(8,128)(2,1)}, u32[]{:S(2)}) copy-start(bf16[256,6144]{1,0:T(8,128)(2,1)} %param.16) | copy-start | bytes 9437188
  7.2 215.0 %reduce-scatter.4.cloned.1.call-start = ((), (), s32[]{:S(2)}) async-start(), calls=%async_computation.1 | async-start | bytes 3244032
  8.8 28.5 %copy-start.6 = (pred[2]{0:T(512)(128)(4,1)}, pred[2]{0:T(512)(128)(4,1)S(1)}, u32[]{:S(2)}) copy-start(pred[2]{0:T(512)(128)(4,1)S(1)} %get-tuple-element.25) | copy-start | bytes 10
  10.5 45.3 %collective-permute-start = (bf16[2,2,128,128]{3,2,0,1:T(8,128)(2,1)S(1)}, bf16[2,2,128,128]{3,2,0,1:T(8,128)(2,1)}, u32[]{:S(2)}, u32[]{:S(2)}) collective-permute-start(bf16[2,2,128,128]{3,2,0,1:T(8,128)(2,1)S(1)} %select_bitcast_fusion.2), channel_id=1, source_target_pairs={{0,8},{1,9},{2,10},{3,11},{4,12},{5,13},{6,14},{7,15},{8,16},{9,17... | collective-permute-start | bytes 393224 | tf_op jit(solution)/shard_map/ppermute | solution.py:16
  16.9 39.0 %collective-permute-start.1 = (bf16[2,2,128,128]{3,2,0,1:T(8,128)(2,1)}, bf16[2,2,128,128]{3,2,0,1:T(8,128)(2,1)}, u32[]{:S(2)}, u32[]{:S(2)}) collective-permute-start(bf16[2,2,128,128]{3,2,0,1:T(8,128)(2,1)} %select_bitcast_fusion.1), channel_id=1, source_target_pairs={{0,16},{1,17},{2,18},{3,19},{4,20},{5,21},{6,22},{7,23},{8,24},{9,... | collective-permute-start | bytes 393224 | tf_op jit(solution)/shard_map/ppermute | solution.py:16
  23.1 23.6 %collective-permute-start.3 = (bf16[3,2,2,128]{3,1,0,2:T(2,128)(2,1)}, bf16[3,2,2,128]{3,1,0,2:T(2,128)(2,1)}, u32[]{:S(2)}, u32[]{:S(2)}) collective-permute-start(bf16[3,2,2,128]{3,1,0,2:T(2,128)(2,1)} %fusion.18), channel_id=1, source_target_pairs={{0,8},{1,9},{2,10},{3,11},{4,12},{5,13},{6,14},{7,15},{8,16},{9,17... | collective-permute-start | bytes 9224 | tf_op jit(solution)/shard_map/ppermute | solution.py:16
  26.2 22.6 %collective-permute-start.4 = (bf16[3,2,2,128]{3,1,0,2:T(2,128)(2,1)}, bf16[3,2,2,128]{3,1,0,2:T(2,128)(2,1)}, u32[]{:S(2)}, u32[]{:S(2)}) collective-permute-start(bf16[3,2,2,128]{3,1,0,2:T(2,128)(2,1)} %fusion.19), channel_id=1, source_target_pairs={{0,16},{1,17},{2,18},{3,19},{4,20},{5,21},{6,22},{7,23},{8,24},{9,... | collective-permute-start | bytes 9224 | tf_op jit(solution)/shard_map/ppermute | solution.py:16
  30.7 18.2 %collective-permute-start.5 = (bf16[3,2,2,128]{3,1,0,2:T(2,128)(2,1)}, bf16[3,2,2,128]{3,1,0,2:T(2,128)(2,1)}, u32[]{:S(2)}, u32[]{:S(2)}) collective-permute-start(bf16[3,2,2,128]{3,1,0,2:T(2,128)(2,1)} %fusion.20), channel_id=1, source_target_pairs={{0,24},{1,25},{2,26},{3,27},{4,28},{5,29},{6,30},{7,31},{8,0},{9,1... | collective-permute-start | bytes 9224 | tf_op jit(solution)/shard_map/ppermute | solution.py:16
  37.3 0.6 copy-start.4
  46.7 9.2 %collective-permute-start.2 = (bf16[2,2,128,128]{3,2,0,1:T(8,128)(2,1)}, bf16[2,2,128,128]{3,2,0,1:T(8,128)(2,1)S(1)}, u32[]{:S(2)}, u32[]{:S(2)}) collective-permute-start(bf16[2,2,128,128]{3,2,0,1:T(8,128)(2,1)} %select_bitcast_fusion), channel_id=1, source_target_pairs={{0,24},{1,25},{2,26},{3,27},{4,28},{5,29},{6,30},{7,31},{8,0},{9,1... | collective-permute-start | bytes 393224 | tf_op jit(solution)/shard_map/ppermute | solution.py:16
  51.7 0.6 copy-start.10
  55.8 4.5 %copy-start.5 = (pred[4]{0:T(512)(128)(4,1)S(1)}, pred[4]{0:T(512)(128)(4,1)}, u32[]{:S(2)}) copy-start(pred[4]{0:T(512)(128)(4,1)} %compare_and_fusion.4) | copy-start | bytes 16
  55.8 5.7 %copy-start.11 = (bf16[4,2,2,128]{3,1,2,0:T(2,128)(2,1)S(1)}, bf16[4,2,2,128]{3,1,2,0:T(2,128)(2,1)}, u32[]{:S(2)}) copy-start(bf16[4,2,2,128]{3,1,2,0:T(2,128)(2,1)} %copy-done.10) | copy-start | bytes 12292
  55.8 6.7 %copy-start.3 = (pred[4,128]{1,0:T(4,128)(4,1)S(1)}, pred[4,128]{1,0:T(4,128)(4,1)}, u32[]{:S(2)}) copy-start(pred[4,128]{1,0:T(4,128)(4,1)} %iota_compare_fusion) | copy-start | bytes 1540
  55.8 6.8 %copy-start.9 = (f32[4,2]{0,1:T(2,128)S(1)}, f32[4,2]{0,1:T(2,128)}, u32[]{:S(2)}) copy-start(f32[4,2]{0,1:T(2,128)} %get-tuple-element.29) | copy-start | bytes 100
  55.8 6.8 %copy-start.2 = (f32[4,2,1,2]{0,3,1,2:T(2,128)S(1)}, f32[4,2,1,2]{0,3,1,2:T(2,128)}, u32[]{:S(2)}) copy-start(f32[4,2,1,2]{0,3,1,2:T(2,128)} %copy.24) | copy-start | bytes 196
  55.8 6.8 %copy-start.13 = (pred[2]{0:T(512)(128)(4,1)S(1)}, pred[2]{0:T(512)(128)(4,1)}, u32[]{:S(2)}) copy-start(pred[2]{0:T(512)(128)(4,1)} %iota_compare_fusion.2) | copy-start | bytes 10
  55.9 7.1 %copy-start.8 = (f32[4,2]{0,1:T(2,128)S(1)}, f32[4,2]{0,1:T(2,128)}, u32[]{:S(2)}) copy-start(f32[4,2]{0,1:T(2,128)} %get-tuple-element.30) | copy-start | bytes 100
  55.9 7.1 %copy-start.12 = (pred[2]{0:T(512)(128)(4,1)S(1)}, pred[2]{0:T(512)(128)(4,1)}, u32[]{:S(2)}) copy-start(pred[2]{0:T(512)(128)(4,1)} %iota_compare_fusion.1) | copy-start | bytes 10
  61.5 0.8 copy-start.1
  69.2 0.7 copy-start.7
Sparse Core Ops, SparseCore 0:
  69.3 152.7 reduce-scatter.3
where the time goes:
time: 412 us; the launch traced here: 411 us
  blocking collectives  179 us (43%)
  waiting for transfers between devices  149 us (36%)
  local copies, waits for them, and re-layouts  22.3 us (5%)
  other arithmetic  20 us (5%)
  starting transfers between devices  19.4 us (5%)
  between operations  14.5 us (4%)
  matrix products  6.82 us (2%)
    unnamed x2, waiting for transfers between devices  149 us
    psum x1, blocking collectives, body(): total = lax.psum(jnp.sum(values, axis=-1), 'head')  71.8 us
    psum x1, blocking collectives, body(): spread = lax.psum(jnp.sum((values - mean) ** 2, axis=-1), 'head')  68.7 us
    all_gather x1, blocking collectives, body(): normed_full = lax.all_gather(normed_part, 'head', axis=1, tiled=True)  38.4 us
    ppermute x6, starting transfers between devices, shifted(): lax.ppermute(shard, axis, [(i, (i + by) % length) for i in range(length)])  19.4 us
  transfers between devices with their start and end apart: 7, of which 1 were waited for; matrix products, arithmetic and copies ran while one was open for 7% of the time, Pallas kernels for 0%

commit v1 on v0

v1 whole, which is shorter than its diff:
```python
import math

import jax
import jax.numpy as jnp
from jax import lax
from jax.experimental import pallas as pl
from jax.experimental.pallas import tpu as pltpu
from jax.sharding import PartitionSpec as P

ROWS = 4
HEAD_DEV = 2
HEAD_DIM = 128
SLOTS = 8
LEN = 128
OUT = 6144
MEMBERS = 32
OLD = MEMBERS // ROWS
SHARE = OUT // MEMBERS
F32 = jnp.float32
BF16 = jnp.bfloat16


def attend_kernel(slot_ref, len_ref, cache_ref, fresh_ref, att_ref, kv_ref, att_scr, sems):
    me = lax.axis_index("head")
    row = me // OLD
    lane = me % OLD
    copies = []
    for target in range(ROWS):
        for i in range(HEAD_DEV):
            slot = slot_ref[(target * OLD + lane) * HEAD_DEV + i]
            for kind in range(2):
                copy = pltpu.make_async_copy(
                    cache_ref.at[0, kind, slot], kv_ref.at[target, kind, i], sems.at[len(copies)]
                )
                copy.start()
                copies.append(copy)
    length = len_ref[row]
    scale = 1.0 / math.sqrt(HEAD_DIM)
    query_rows, old_scores, new_first, new_second = [], [], [], []
    odd = lax.broadcasted_iota(jnp.int32, (8, HEAD_DIM), 0) % 2 == 1
    fresh = fresh_ref[0].astype(F32)
    for slot in range(SLOTS):
        query = jnp.where(
            odd,
            jnp.broadcast_to(fresh[0, 1, slot : slot + 1], (8, HEAD_DIM)),
            jnp.broadcast_to(fresh[0, 0, slot : slot + 1], (8, HEAD_DIM)),
        )
        query_rows.append(query)
        old_scores.append(
            lax.dot_general(
                query.astype(BF16),
                cache_ref[0, 0, slot],
                (((1,), (1,)), ((), ())),
                preferred_element_type=F32,
            )
        )
        new_first.append(jnp.sum(query * fresh[1, 0, slot : slot + 1], axis=-1, keepdims=True))
        new_second.append(jnp.sum(query * fresh[1, 1, slot : slot + 1], axis=-1, keepdims=True))
    shape = (SLOTS * 8, LEN)
    scores = jnp.concatenate(old_scores, axis=0) * scale
    first = jnp.concatenate(new_first, axis=0) * scale
    second = jnp.concatenate(new_second, axis=0) * scale
    visible = lax.broadcasted_iota(jnp.int32, shape, 1) < length
    later = lax.broadcasted_iota(jnp.int32, (SLOTS * 8, 1), 0) % 2 == 1
    scores = jnp.where(visible, scores, -1e30)
    second = jnp.where(later, second, -1e30)
    top = jnp.maximum(jnp.max(scores, axis=-1, keepdims=True), jnp.maximum(first, second))
    old_exp = jnp.where(visible, jnp.exp(scores - top), 0.0)
    first_exp = jnp.exp(first - top)
    second_exp = jnp.where(later, jnp.exp(second - top), 0.0)
    total = jnp.sum(old_exp, axis=-1, keepdims=True) + first_exp + second_exp
    old_w = (old_exp / total).astype(BF16)
    first_w = (first_exp / total).astype(BF16).astype(F32)
    second_w = (second_exp / total).astype(BF16).astype(F32)
    mine = lax.broadcasted_iota(jnp.int32, (8, HEAD_DIM), 0) // 2 == row
    for slot in range(SLOTS):
        part = slice(slot * 8, slot * 8 + 8)
        result = jnp.dot(old_w[part], cache_ref[0, 1, slot], preferred_element_type=F32)
        result = result + (
            first_w[part] * fresh[2, 0, slot : slot + 1]
            + second_w[part] * fresh[2, 1, slot : slot + 1]
        )
        att_scr[slot] = jnp.where(mine, result, 0.0)
    for target in range(ROWS):
        pair = [
            att_scr[slot_ref[(target * OLD + lane) * HEAD_DEV + i]] for i in range(HEAD_DEV)
        ]
        att_ref[target] = jnp.concatenate(pair, axis=0).astype(BF16)
    for copy in copies:
        copy.wait()


def attend_and_pick(slot_map, lengths, cache, fresh):
    smem = pl.BlockSpec(memory_space=pltpu.SMEM)
    vmem = pl.BlockSpec(memory_space=pltpu.VMEM)
    return pl.pallas_call(
        attend_kernel,
        out_shape=(
            jax.ShapeDtypeStruct((ROWS, HEAD_DEV * 8, HEAD_DIM), BF16),
            jax.ShapeDtypeStruct((ROWS, 2, HEAD_DEV, LEN, HEAD_DIM), BF16),
        ),
        in_specs=[smem, smem, vmem, vmem],
        out_specs=(vmem, pl.BlockSpec(memory_space=pl.ANY)),
        scratch_shapes=[
            pltpu.VMEM((SLOTS, 8, HEAD_DIM), F32),
            pltpu.SemaphoreType.DMA((ROWS * HEAD_DEV * 2,)),
        ],
        compiler_params=pltpu.CompilerParams(vmem_limit_bytes=16 * 2**20),
        name="attend_and_pick",
    )(slot_map, lengths, cache, fresh)


CHUNK = 2 * SHARE
CHUNKS = OUT // CHUNK


def project_kernel(att_ref, weight_ref, out_ref):
    total = att_ref[0].astype(F32)
    for row in range(1, ROWS):
        total = total + att_ref[row].astype(F32)
    features = jnp.concatenate([total[:8], total[8:]], axis=1).astype(BF16)
    for chunk in range(CHUNKS):
        part = jnp.dot(
            features,
            weight_ref[:, chunk * CHUNK : (chunk + 1) * CHUNK],
            preferred_element_type=F32,
        )
        out_ref[2 * chunk] = part[:, :SHARE].astype(BF16)
        out_ref[2 * chunk + 1] = part[:, SHARE:].astype(BF16)


def project(attended, out_weight):
    vmem = pl.BlockSpec(memory_space=pltpu.VMEM)
    return pl.pallas_call(
        project_kernel,
        out_shape=jax.ShapeDtypeStruct((MEMBERS, 8, SHARE), BF16),
        in_specs=[vmem, vmem],
        out_specs=vmem,
        compiler_params=pltpu.CompilerParams(vmem_limit_bytes=16 * 2**20),
        name="project",
    )(attended, out_weight)


def add_kernel(parts_ref, residual_ref, hidden_ref, spread_ref):
    total = parts_ref[0].astype(F32)
    for member in range(1, MEMBERS):
        total = total + parts_ref[member].astype(F32)
    hidden = (residual_ref[...].astype(F32) + total).astype(BF16)
    hidden_ref[...] = hidden
    for member in range(MEMBERS):
        spread_ref[member] = hidden


def add_residual(parts, residual):
    vmem = pl.BlockSpec(memory_space=pltpu.VMEM)
    return pl.pallas_call(
        add_kernel,
        out_shape=(
            jax.ShapeDtypeStruct((8, SHARE), BF16),
            jax.ShapeDtypeStruct((MEMBERS, 8, SHARE), BF16),
        ),
        in_specs=[vmem, vmem],
        out_specs=(vmem, vmem),
        compiler_params=pltpu.CompilerParams(vmem_limit_bytes=16 * 2**20),
        name="add_residual",
    )(parts, residual)


def norm_kernel(blocks_ref, gain_ref, bias_ref, out_ref):
    total = blocks_ref[0].astype(F32)
    for member in range(1, MEMBERS):
        total = total + blocks_ref[member].astype(F32)
    mean = jnp.sum(total, axis=-1, keepdims=True) / OUT
    spread = jnp.zeros((8, SHARE), F32)
    for member in range(MEMBERS):
        spread = spread + (blocks_ref[member].astype(F32) - mean) ** 2
    var = jnp.sum(spread, axis=-1, keepdims=True) / OUT
    scale = 1.0 / jnp.sqrt(var + 1e-05)
    for chunk in range(CHUNKS):
        values = jnp.concatenate(
            [blocks_ref[2 * chunk].astype(F32), blocks_ref[2 * chunk + 1].astype(F32)], axis=1
        )
        values = (values - mean) * scale
        for tile in range(CHUNK // 128):
            at = chunk * (CHUNK // 128) + tile
            part = values[:, tile * 128 : (tile + 1) * 128]
            part = part * gain_ref[at : at + 1] + bias_ref[at : at + 1]
            out_ref[:, at * 128 : (at + 1) * 128] = part.astype(BF16)


def normalize(blocks, gain, bias):
    vmem = pl.BlockSpec(memory_space=pltpu.VMEM)
    return pl.pallas_call(
        norm_kernel,
        out_shape=jax.ShapeDtypeStruct((8, OUT), BF16),
        in_specs=[vmem, vmem, vmem],
        out_specs=vmem,
        compiler_params=pltpu.CompilerParams(vmem_limit_bytes=16 * 2**20),
        name="normalize",
    )(blocks, gain.reshape(OUT // 128, 128), bias.reshape(OUT // 128, 128))


def exchange(blocks, groups=None):
    return lax.all_to_all(blocks, "head", 0, 0, axis_index_groups=groups, tiled=True)


def body(cache, fresh, slot_map, lengths, out_weight, residual, norm_gain, norm_bias):
    columns = [[row * OLD + lane for row in range(ROWS)] for lane in range(OLD)]
    picked, kv_blocks = attend_and_pick(slot_map, lengths, cache, fresh)
    attended = exchange(picked, columns)
    cache_new = exchange(kv_blocks, columns)[None]
    parts = exchange(project(attended, out_weight))
    hidden, copies = add_residual(parts, residual.reshape(ROWS * 2, SHARE))
    normed = normalize(exchange(copies), norm_gain, norm_bias)
    return (cache_new, hidden.reshape(ROWS, 2, SHARE), normed.reshape(ROWS, 2, OUT))


def solution(mesh):
    in_specs = (
        P(("grp", "head"), None, None, None, None),
        P(("grp", "head"), None, None, None, None),
        P("grp"),
        P("grp"),
        P("head", None),
        P("grp", None, "head"),
        P(),
        P(),
    )
    out_specs = (
        P(("grp", "head"), None, None, None, None, None),
        P("grp", None, "head"),
        P("grp", None, None),
    )
    return jax.shard_map(body, mesh=mesh, in_specs=in_specs, out_specs=out_specs, check_vma=False)
```

time: 412 us -> 66.9 us (0.16)
  blocking collectives: 179 us -> 21.7 us
  waiting for transfers between devices: 149 us -> 21.2 us
  other arithmetic: 20 us -> 0 us
  local copies, waits for them, and re-layouts: 22.3 us -> 7.08 us
  between operations: 14.5 us -> 0.69 us
  starting transfers between devices: 19.4 us -> 12.1 us
  matrix products: 6.82 us -> 0 us
    unnamed x2 -> x0, waiting for transfers between devices: 149 us -> none
    psum x2 -> x0, blocking collectives: 140 us -> none  [the longest x1 71.8 us: body(): total = lax.psum(jnp.sum(values, axis=-1), 'head')]
    all_gather x1 -> x0, blocking collectives: 38.4 us -> none  [body(): normed_full = lax.all_gather(normed_part, 'head', axis=1, tiled=True)]
    all_to_all x0 -> x2, blocking collectives: none -> 21.7 us  [exchange(): lax.all_to_all(blocks, 'head', 0, 0, axis_index_groups=groups, tiled=True)]
    all_to_all x0 -> x2, waiting for transfers between devices: none -> 21.2 us  [exchange(): lax.all_to_all(blocks, 'head', 0, 0, axis_index_groups=groups, tiled=True)]
    ppermute x6 -> x0, starting transfers between devices: 19.4 us -> none  [shifted(): lax.ppermute(shard, axis, [(i, (i + by) % length) for i in range(length)])]
    gather x10 -> x0, local copies, waits for them, and re-layouts: 12.7 us -> none  [the longest x4 6.46 us: select_heads(): jnp.take(cache[0], wanted, axis=1)]
    all_to_all x0 -> x2, starting transfers between devices: none -> 12.1 us  [exchange(): lax.all_to_all(blocks, 'head', 0, 0, axis_index_groups=groups, tiled=True)]
  transfers between devices with their start and end apart: 7 -> 2, of which waited for: 1 -> 2; matrix products, arithmetic and copies ran while one was open for 7% -> 2% of each run, Pallas kernels for 0% -> 0%
where the time goes in v1:
time: 66.9 us; the launch traced here: 66.4 us
  blocking collectives  21.7 us (32%)
  waiting for transfers between devices  21.2 us (32%)
  starting transfers between devices  12.1 us (18%)
  local copies, waits for them, and re-layouts  7.08 us (11%)
  Pallas kernels  3.58 us (5%)
  between operations  0.69 us (1%)
    all_to_all x2, blocking collectives, exchange(): lax.all_to_all(blocks, 'head', 0, 0, axis_index_groups=groups, tiled=True)  21.7 us
    all_to_all x2, waiting for transfers between devices, exchange(): lax.all_to_all(blocks, 'head', 0, 0, axis_index_groups=groups, tiled=True)  21.2 us
    all_to_all x2, starting transfers between devices, exchange(): lax.all_to_all(blocks, 'head', 0, 0, axis_index_groups=groups, tiled=True)  12.1 us
    unnamed x17, local copies, waits for them, and re-layouts  5.74 us
    pallas_call x1, Pallas kernels, attend_and_pick(): pl.pallas_call(attend_kernel, out_shape=(jax.ShapeDtypeStruct((ROWS, HEAD...  2.02 us
  transfers between devices with their start and end apart: 2, of which 2 were waited for; matrix products, arithmetic and copies ran while one was open for 2% of the time, Pallas kernels for 0%

profile of v1, /device:TPU:1, one launch (start us, length us, event | category | flops | bytes accessed | tf_op | source)
XLA Modules:
  0.0 66.4 jit_solution(1693925250446653978)
XLA Ops:
  0.6 0.0 copy-start.1
  0.6 1.0 %copy-done.1 = bf16[1,2,8,128,128]{4,3,2,1,0:T(8,128)(2,1)S(1)} copy-done((bf16[1,2,8,128,128]{4,3,2,1,0:T(8,128)(2,1)S(1)}, bf16[1,2,8,128,128]{4,3,2,1,0:T(8,128)(2,1)}, u32[]{:S(2)}) %copy-start.1) | copy-done | bytes 524312
  1.7 0.0 copy-start.4
  1.7 0.7 %copy-done.4 = bf16[1,3,2,8,128]{4,3,2,1,0:T(8,128)(2,1)S(1)} copy-done((bf16[1,3,2,8,128]{4,3,2,1,0:T(8,128)(2,1)S(1)}, bf16[1,3,2,8,128]{4,3,2,1,0:T(8,128)(2,1)}, u32[]{:S(2)}) %copy-start.4) | copy-done | bytes 12312
  2.4 0.0 copy-start.5
  2.4 0.7 copy-done.5
  3.0 0.0 copy-start.6
  3.0 0.7 copy-done.6
  3.7 0.0 copy-start.7
  3.7 0.0 copy-start.2
  3.7 0.0 copy-start.3
  3.7 2.0 %attend_and_pick.1 = (bf16[4,16,128]{2,1,0:T(8,128)(2,1)S(1)}, bf16[4,2,2,128,128]{4,3,2,1,0:T(8,128)(2,1)}) custom-call(s32[64]{0:T(128)S(1)} %copy-done.5, s32[4]{0:T(128)S(1)} %copy-done.6, bf16[1,2,8,128,128]{4,3,2,1,0:T(8,128)(2,1)S(1)} %copy-done.1, bf16[1,3,2,8,128]{4,3,2,1,0:T(8,128)(2,1)S(1)} %copy-done.4), custom_call_target="tpu_custom_call" | custom-call | tf_op jit(solution)/shard_map/attend_and_pick/pallas_call | solution.py:96
  5.7 9.7 %all_to_all.20.att_ref = bf16[4,16,128]{2,1,0:T(8,128)(2,1)S(1)} all-to-all(bf16[4,16,128]{2,1,0:T(8,128)(2,1)S(1)} %get-tuple-element.8), channel_id=1, replica_groups={{0,8,16,24},{1,9,17,25},{2,10,18,26},{3,11,19,27},{4,12,20,28},{5,13,21..., dimensions={0} | all-to-all | bytes 32768 | tf_op jit(solution)/shard_map/all_to_all | solution.py:204
  15.4 0.0 copy-start
  15.4 1.9 %copy-done = bf16[256,6144]{1,0:T(8,128)(2,1)S(1)} copy-done((bf16[256,6144]{1,0:T(8,128)(2,1)S(1)}, bf16[256,6144]{1,0:T(8,128)(2,1)}, u32[]{:S(2)}) %copy-start) | copy-done | bytes 3145752
  17.3 1.2 %project.1 = bf16[32,8,192]{2,1,0:T(8,128)(2,1)} custom-call(bf16[4,16,128]{2,1,0:T(8,128)(2,1)S(1)} %all_to_all.20.att_ref, bf16[256,6144]{1,0:T(8,128)(2,1)S(1)} %copy-done), custom_call_target="tpu_custom_call" | custom-call | tf_op jit(solution)/shard_map/project/pallas_call | solution.py:134
  18.6 8.7 %all-to-all-start.2 = ((bf16[32,8,192]{2,1,0:T(8,128)(2,1)}), bf16[32,8,192]{2,1,0:T(8,128)(2,1)S(1)}, u32[]{:S(2)}, u32[]{:S(2)}) async-start(bf16[32,8,192]{2,1,0:T(8,128)(2,1)} %project.1), calls=%async_computation.2 | async-start | bytes 262144 | tf_op jit(solution)/shard_map/all_to_all | solution.py:204
  27.2 0.0 copy-done.7
  27.2 8.6 %all-to-all-done.2.parts_ref = bf16[32,8,192]{2,1,0:T(8,128)(2,1)S(1)} async-done(((bf16[32,8,192]{2,1,0:T(8,128)(2,1)}), bf16[32,8,192]{2,1,0:T(8,128)(2,1)S(1)}, u32[]{:S(2)}, u32[]{:S(2)}) %all-to-all-start.2) | async-done | bytes 98336 | tf_op jit(solution)/shard_map/all_to_all | solution.py:204
  35.9 12.0 %all_to_all.21.blocks_ref = bf16[32,8,192]{2,1,0:T(8,128)(2,1)S(1)} all-to-all(bf16[32,8,192]{2,1,0:T(8,128)(2,1)S(1)} %get-tuple-element.10), channel_id=1, replica_groups=mesh['grp'=16,'head'=32] {'head'}, dimensions={0} | all-to-all | bytes 196608 | tf_op jit(solution)/shard_map/all_to_all | solution.py:204
  48.0 3.5 %all-to-all-start = ((bf16[4,2,2,128,128]{4,3,2,1,0:T(8,128)(2,1)}), bf16[4,2,2,128,128]{4,3,2,1,0:T(8,128)(2,1)S(1)}, u32[]{:S(2)}, u32[]{:S(2)}) async-start(bf16[4,2,2,128,128]{4,3,2,1,0:T(8,128)(2,1)} %get-tuple-element.7), calls=%async_computation | async-start | bytes 1048576 | tf_op jit(solution)/shard_map/all_to_all | solution.py:204
  51.4 0.6 reshape.22
  52.0 0.0 copy-done.2
  52.0 0.0 copy-done.3
  52.0 0.3 normalize.1
  52.3 0.7 %reshape.25 = bf16[4,2,6144]{2,1,0:T(2,128)(2,1)} reshape(bf16[8,6144]{1,0:T(8,128)(2,1)S(1)} %normalize.1) | data formatting | bytes 196608 | tf_op jit(solution)/shard_map/reshape | solution.py:215
  53.0 12.6 %all-to-all-done = bf16[4,2,2,128,128]{4,3,2,1,0:T(8,128)(2,1)S(1)} async-done(((bf16[4,2,2,128,128]{4,3,2,1,0:T(8,128)(2,1)}), bf16[4,2,2,128,128]{4,3,2,1,0:T(8,128)(2,1)S(1)}, u32[]{:S(2)}, u32[]{:S(2)}) %all-to-all-start) | async-done | bytes 524320 | tf_op jit(solution)/shard_map/all_to_all | solution.py:204
  65.6 0.8 %copy.12 = bf16[1,4,2,2,128,128]{5,4,3,2,1,0:T(8,128)(2,1)} copy(bf16[1,4,2,2,128,128]{5,4,3,2,1,0:T(8,128)(2,1)S(1)} %bitcast.5) | data formatting | bytes 1048576
  (2 shorter events, 0.1 us)
Async XLA Ops:
  0.6 1.0 %copy-start.1 = (bf16[1,2,8,128,128]{4,3,2,1,0:T(8,128)(2,1)S(1)}, bf16[1,2,8,128,128]{4,3,2,1,0:T(8,128)(2,1)}, u32[]{:S(2)}) copy-start(bf16[1,2,8,128,128]{4,3,2,1,0:T(8,128)(2,1)} %cache_ref.1) | copy-start | bytes 1572868
  1.7 0.7 %copy-start.4 = (bf16[1,3,2,8,128]{4,3,2,1,0:T(8,128)(2,1)S(1)}, bf16[1,3,2,8,128]{4,3,2,1,0:T(8,128)(2,1)}, u32[]{:S(2)}) copy-start(bf16[1,3,2,8,128]{4,3,2,1,0:T(8,128)(2,1)} %fresh_ref.1) | copy-start | bytes 36868
  2.4 0.7 copy-start.5
  3.0 0.7 copy-start.6
  3.7 23.5 %copy-start.7 = (bf16[4,2,192]{2,1,0:T(2,128)(2,1)S(1)}, bf16[4,2,192]{2,1,0:T(2,128)(2,1)}, u32[]{:S(2)}) copy-start(bf16[4,2,192]{2,1,0:T(2,128)(2,1)} %param.13) | copy-start | bytes 9220
  3.7 48.3 %copy-start.2 = (f32[6144]{0:T(1024)S(1)}, f32[6144]{0:T(1024)}, u32[]{:S(2)}) copy-start(f32[6144]{0:T(1024)} %param.14) | copy-start | bytes 73732
  3.7 48.3 %copy-start.3 = (f32[6144]{0:T(1024)S(1)}, f32[6144]{0:T(1024)}, u32[]{:S(2)}) copy-start(f32[6144]{0:T(1024)} %param.15) | copy-start | bytes 73732
  15.4 1.9 %copy-start = (bf16[256,6144]{1,0:T(8,128)(2,1)S(1)}, bf16[256,6144]{1,0:T(8,128)(2,1)}, u32[]{:S(2)}) copy-start(bf16[256,6144]{1,0:T(8,128)(2,1)} %weight_ref.1) | copy-start | bytes 9437188
  18.6 17.3 %all-to-all-start.2 = ((bf16[32,8,192]{2,1,0:T(8,128)(2,1)}), bf16[32,8,192]{2,1,0:T(8,128)(2,1)S(1)}, u32[]{:S(2)}, u32[]{:S(2)}) async-start(bf16[32,8,192]{2,1,0:T(8,128)(2,1)} %project.1), calls=%async_computation.2 | async-start | bytes 262144 | tf_op jit(solution)/shard_map/all_to_all | solution.py:204
  48.0 17.7 %all-to-all-start = ((bf16[4,2,2,128,128]{4,3,2,1,0:T(8,128)(2,1)}), bf16[4,2,2,128,128]{4,3,2,1,0:T(8,128)(2,1)S(1)}, u32[]{:S(2)}, u32[]{:S(2)}) async-start(bf16[4,2,2,128,128]{4,3,2,1,0:T(8,128)(2,1)} %get-tuple-element.7), calls=%async_computation | async-start | bytes 1048576 | tf_op jit(solution)/shard_map/all_to_all | solution.py:204

commit v2 on v1

v2 whole, which is shorter than its diff:
```python
import math

import jax
import jax.numpy as jnp
from jax import lax
from jax.experimental import pallas as pl
from jax.experimental.pallas import tpu as pltpu
from jax.sharding import PartitionSpec as P

ROWS = 4
HEAD_DEV = 2
HEAD_DIM = 128
SLOTS = 8
LEN = 128
OUT = 6144
MEMBERS = 32
CORES = 2
CHIPS = MEMBERS // CORES
OLD = MEMBERS // ROWS
SHARE = OUT // MEMBERS
CHUNK = OUT // CHIPS
F32 = jnp.float32
BF16 = jnp.bfloat16
FIRST_LIMIT = 56 * 2**20
VMEM_LIMIT = 8 * 2**20
SMEM = pl.BlockSpec(memory_space=pltpu.SMEM)
VMEM = pl.BlockSpec(memory_space=pltpu.VMEM)
ANY = pl.BlockSpec(memory_space=pl.ANY)


def attend_kernel(
    slot_ref, len_ref, cache_ref, fresh_ref, att_ref, new_ref, kv1, kv2, kv3, held, att_scr, in_sems, sems
):
    me = lax.axis_index("head")
    row = me // OLD
    lane = me % OLD
    loads = []
    for kind in range(2):
        load = pltpu.make_async_copy(cache_ref.at[0, kind], held.at[kind], in_sems.at[kind])
        load.start()
        loads.append(load)
    copies = []

    def pick(kind):
        for offset, kv_ref in ((1, kv1), (2, kv2), (3, kv3), (0, new_ref.at[0, row])):
            target = (row + offset) % ROWS
            for i in range(HEAD_DEV):
                slot = slot_ref[(target * OLD + lane) * HEAD_DEV + i]
                copy = pltpu.make_async_copy(
                    held.at[kind, slot], kv_ref.at[kind, i], sems.at[len(copies)]
                )
                copy.start()
                copies.append(copy)

    length = len_ref[row]
    scale = 1.0 / math.sqrt(HEAD_DIM)
    query_rows, old_scores, new_first, new_second = [], [], [], []
    odd = lax.broadcasted_iota(jnp.int32, (8, HEAD_DIM), 0) % 2 == 1
    fresh = fresh_ref[0].astype(F32)
    for slot in range(SLOTS):
        query = jnp.where(
            odd,
            jnp.broadcast_to(fresh[0, 1, slot : slot + 1], (8, HEAD_DIM)),
            jnp.broadcast_to(fresh[0, 0, slot : slot + 1], (8, HEAD_DIM)),
        )
        query_rows.append(query.astype(BF16))
        new_first.append(jnp.sum(query * fresh[1, 0, slot : slot + 1], axis=-1, keepdims=True))
        new_second.append(jnp.sum(query * fresh[1, 1, slot : slot + 1], axis=-1, keepdims=True))
    loads[0].wait()
    pick(0)
    for slot in range(SLOTS):
        old_scores.append(
            lax.dot_general(
                query_rows[slot],
                held[0, slot],
                (((1,), (1,)), ((), ())),
                preferred_element_type=F32,
            )
        )
    shape = (SLOTS * 8, LEN)
    scores = jnp.concatenate(old_scores, axis=0) * scale
    first = jnp.concatenate(new_first, axis=0) * scale
    second = jnp.concatenate(new_second, axis=0) * scale
    visible = lax.broadcasted_iota(jnp.int32, shape, 1) < length
    later = lax.broadcasted_iota(jnp.int32, (SLOTS * 8, 1), 0) % 2 == 1
    scores = jnp.where(visible, scores, -1e30)
    second = jnp.where(later, second, -1e30)
    top = jnp.maximum(jnp.max(scores, axis=-1, keepdims=True), jnp.maximum(first, second))
    old_exp = jnp.where(visible, jnp.exp(scores - top), 0.0)
    first_exp = jnp.exp(first - top)
    second_exp = jnp.where(later, jnp.exp(second - top), 0.0)
    total = jnp.sum(old_exp, axis=-1, keepdims=True) + first_exp + second_exp
    old_w = (old_exp / total).astype(BF16)
    first_w = (first_exp / total).astype(BF16).astype(F32)
    second_w = (second_exp / total).astype(BF16).astype(F32)
    mine = lax.broadcasted_iota(jnp.int32, (8, HEAD_DIM), 0) // 2 == row
    loads[1].wait()
    pick(1)
    for slot in range(SLOTS):
        part = slice(slot * 8, slot * 8 + 8)
        result = jnp.dot(old_w[part], held[1, slot], preferred_element_type=F32)
        result = result + (
            first_w[part] * fresh[2, 0, slot : slot + 1]
            + second_w[part] * fresh[2, 1, slot : slot + 1]
        )
        att_scr[slot] = jnp.where(mine, result, 0.0)
    for target in range(ROWS):
        pair = [
            att_scr[slot_ref[(target * OLD + lane) * HEAD_DEV + i]] for i in range(HEAD_DEV)
        ]
        att_ref[target] = jnp.concatenate(pair, axis=0).astype(BF16)
    for copy in copies:
        copy.wait()


def attend_and_pick(slot_map, lengths, cache, fresh):
    block = (2, HEAD_DEV, LEN, HEAD_DIM)
    return pl.pallas_call(
        attend_kernel,
        out_shape=(
            jax.ShapeDtypeStruct((ROWS, HEAD_DEV * 8, HEAD_DIM), BF16),
            jax.ShapeDtypeStruct((1, ROWS) + block, BF16),
            *[jax.ShapeDtypeStruct(block, BF16)] * (ROWS - 1),
        ),
        in_specs=[SMEM, SMEM, ANY, VMEM],
        out_specs=(VMEM, *[ANY] * ROWS),
        scratch_shapes=[
            pltpu.VMEM((2, SLOTS, LEN, HEAD_DIM), BF16),
            pltpu.VMEM((SLOTS, 8, HEAD_DIM), F32),
            pltpu.SemaphoreType.DMA((2,)),
            pltpu.SemaphoreType.DMA((ROWS * HEAD_DEV * 2,)),
        ],
        compiler_params=pltpu.CompilerParams(vmem_limit_bytes=FIRST_LIMIT),
        name="attend_and_pick",
    )(slot_map, lengths, cache, fresh)


def project_kernel(att_ref, weight_ref, out_ref):
    total = att_ref[0].astype(F32)
    for row in range(1, ROWS):
        total = total + att_ref[row].astype(F32)
    features = jnp.concatenate([total[:8], total[8:]], axis=1).astype(BF16)
    for chip in range(CHIPS):
        part = jnp.dot(
            features,
            weight_ref[:, chip * CHUNK : (chip + 1) * CHUNK],
            preferred_element_type=F32,
        )
        out_ref[chip] = part.astype(BF16)


def project(attended, out_weight):
    return pl.pallas_call(
        project_kernel,
        out_shape=jax.ShapeDtypeStruct((CHIPS, 8, CHUNK), BF16),
        in_specs=[VMEM, VMEM],
        out_specs=VMEM,
        compiler_params=pltpu.CompilerParams(vmem_limit_bytes=VMEM_LIMIT),
        name="project",
    )(attended, out_weight)


def add_kernel(parts_ref, residual_ref, out_ref):
    core = lax.axis_index("head") % CORES
    total = parts_ref[0].astype(F32)
    for chip in range(1, CHIPS):
        total = total + parts_ref[chip].astype(F32)
    own = jnp.concatenate([residual_ref[row].astype(F32) for row in range(ROWS)], axis=0)
    none = jnp.zeros_like(own)
    own = jnp.concatenate(
        [jnp.where(core == 0, own, none), jnp.where(core == 1, own, none)], axis=1
    )
    out_ref[...] = total + own


def add_residual(parts, residual):
    return pl.pallas_call(
        add_kernel,
        out_shape=jax.ShapeDtypeStruct((8, CHUNK), F32),
        in_specs=[VMEM, VMEM],
        out_specs=VMEM,
        compiler_params=pltpu.CompilerParams(vmem_limit_bytes=VMEM_LIMIT),
        name="add_residual",
    )(parts, residual)


def hidden_kernel(sums_ref, hidden_ref, spread_ref):
    core = lax.axis_index("head") % CORES
    total = sums_ref[0] + sums_ref[1]
    hidden = total.astype(BF16)
    own = jnp.where(core == 0, total[:, :SHARE], total[:, SHARE:]).astype(BF16)
    for row in range(ROWS):
        hidden_ref[row] = own[2 * row : 2 * row + 2]
    for chip in range(CHIPS):
        spread_ref[chip] = hidden


def round_hidden(sums):
    return pl.pallas_call(
        hidden_kernel,
        out_shape=(
            jax.ShapeDtypeStruct((ROWS, 2, SHARE), BF16),
            jax.ShapeDtypeStruct((CHIPS, 8, CHUNK), BF16),
        ),
        in_specs=[VMEM],
        out_specs=(VMEM, VMEM),
        compiler_params=pltpu.CompilerParams(vmem_limit_bytes=VMEM_LIMIT),
        name="round_hidden",
    )(sums)


def norm_kernel(blocks_ref, gain_ref, bias_ref, kv1, kv2, kv3, _, out_ref, cache_ref, sems):
    row = lax.axis_index("head") // OLD
    copies = []
    for offset, kv_ref in enumerate((kv1, kv2, kv3), 1):
        source = (row + ROWS - offset) % ROWS
        copy = pltpu.make_async_copy(kv_ref, cache_ref.at[0, source], sems.at[offset - 1])
        copy.start()
        copies.append(copy)
    total = blocks_ref[0].astype(F32)
    for chip in range(1, CHIPS):
        total = total + blocks_ref[chip].astype(F32)
    mean = jnp.sum(total, axis=-1, keepdims=True) / OUT
    spread = jnp.zeros((8, CHUNK), F32)
    for chip in range(CHIPS):
        spread = spread + (blocks_ref[chip].astype(F32) - mean) ** 2
    var = jnp.sum(spread, axis=-1, keepdims=True) / OUT
    scale = 1.0 / jnp.sqrt(var + 1e-05)
    tiles = CHUNK // 128
    for chip in range(CHIPS):
        values = (blocks_ref[chip].astype(F32) - mean) * scale
        for tile in range(tiles):
            at = chip * tiles + tile
            part = values[:, tile * 128 : (tile + 1) * 128]
            part = (part * gain_ref[at : at + 1] + bias_ref[at : at + 1]).astype(BF16)
            for step in range(ROWS):
                out_ref[step, :, at * 128 : (at + 1) * 128] = part[2 * step : 2 * step + 2]
    for copy in copies:
        copy.wait()


def normalize(blocks, gain, bias, kv, cache_new):
    return pl.pallas_call(
        norm_kernel,
        out_shape=(
            jax.ShapeDtypeStruct((ROWS, 2, OUT), BF16),
            jax.ShapeDtypeStruct(cache_new.shape, BF16),
        ),
        in_specs=[VMEM] * 6 + [ANY],
        out_specs=(VMEM, ANY),
        scratch_shapes=[pltpu.SemaphoreType.DMA((ROWS - 1,))],
        input_output_aliases={6: 1},
        compiler_params=pltpu.CompilerParams(vmem_limit_bytes=VMEM_LIMIT),
        name="normalize",
    )(blocks, gain.reshape(OUT // 128, 128), bias.reshape(OUT // 128, 128), *kv, cache_new)


def exchange(blocks, groups):
    return lax.all_to_all(blocks, "head", 0, 0, axis_index_groups=groups, tiled=True)


def body(cache, fresh, slot_map, lengths, out_weight, residual, norm_gain, norm_bias):
    columns = [[row * OLD + lane for row in range(ROWS)] for lane in range(OLD)]
    sides = [[chip * CORES + core for chip in range(CHIPS)] for core in range(CORES)]
    pairs = [[chip * CORES + core for core in range(CORES)] for chip in range(CHIPS)]
    picked, cache_new, *kv = attend_and_pick(slot_map, lengths, cache, fresh)
    for offset in range(1, ROWS):
        to = [(i, (i + offset * OLD) % MEMBERS) for i in range(MEMBERS)]
        kv[offset - 1] = lax.ppermute(kv[offset - 1], "head", to)
    parts = exchange(project(exchange(picked, columns), out_weight), sides)
    sums = lax.all_gather(add_residual(parts, residual), "head", axis_index_groups=pairs)
    hidden, copies = round_hidden(sums)
    normed, cache_new = normalize(exchange(copies, sides), norm_gain, norm_bias, kv, cache_new)
    return (cache_new, hidden, normed)


def solution(mesh):
    in_specs = (
        P(("grp", "head"), None, None, None, None),
        P(("grp", "head"), None, None, None, None),
        P("grp"),
        P("grp"),
        P("head", None),
        P("grp", None, "head"),
        P(),
        P(),
    )
    out_specs = (
        P(("grp", "head"), None, None, None, None, None),
        P("grp", None, "head"),
        P("grp", None, None),
    )
    return jax.shard_map(body, mesh=mesh, in_specs=in_specs, out_specs=out_specs, check_vma=False)
```

time: 66.9 us -> 57.8 us (0.86)
  waiting for transfers between devices: 21.2 us -> 5.91 us
  blocking collectives: 21.7 us -> 28.5 us
  local copies, waits for them, and re-layouts: 7.08 us -> 1.91 us
  Pallas kernels: 3.58 us -> 6.49 us
  starting transfers between devices: 12.1 us -> 13.8 us
    all_to_all x2 -> x1, waiting for transfers between devices: 21.2 us -> 0.01 us  [exchange(): lax.all_to_all(blocks, 'head', 0, 0, axis_index_groups=groups, tiled=True)]
    ppermute x0 -> x3, starting transfers between devices: none -> 10.3 us  [body(): kv[offset - 1] = lax.ppermute(kv[offset - 1], 'head', to)]
    all_to_all x2 -> x1, starting transfers between devices: 12.1 us -> 3.51 us  [exchange(): lax.all_to_all(blocks, 'head', 0, 0, axis_index_groups=groups, tiled=True)]
    all_gather x0 -> x1, blocking collectives: none -> 6.78 us  [body(): lax.all_gather(add_residual(parts, residual), 'head', axis_index_groups=p...]
    ppermute x0 -> x3, waiting for transfers between devices: none -> 5.91 us  [body(): kv[offset - 1] = lax.ppermute(kv[offset - 1], 'head', to)]
    unnamed x17 -> x14, local copies, waits for them, and re-layouts: 5.74 us -> 1.91 us
    pallas_call x1, Pallas kernels: 2.02 us -> 3.78 us  [attend_and_pick(): pl.pallas_call(attend_kernel, out_shape=(jax.ShapeDtypeStruct((ROWS, HEAD...]
    reshape x3 -> x0, local copies, waits for them, and re-layouts: 1.34 us -> none  [the longest x1 0.72 us: body(): normed.reshape(ROWS, 2, OUT)]
  transfers between devices with their start and end apart: 2 -> 4, of which waited for: 2 -> 2; matrix products, arithmetic and copies ran while one was open for 2% -> 0% of each run, Pallas kernels for 0% -> 0%
where the time goes in v2:
time: 57.8 us; the launch traced here: 57.3 us
  blocking collectives  28.5 us (49%)
  starting transfers between devices  13.8 us (24%)
  Pallas kernels  6.49 us (11%)
  waiting for transfers between devices  5.91 us (10%)
  local copies, waits for them, and re-layouts  1.91 us (3%)
  between operations  0.74 us (1%)
    all_to_all x2, blocking collectives, exchange(): lax.all_to_all(blocks, 'head', 0, 0, axis_index_groups=groups, tiled=True)  21.7 us
    ppermute x3, starting transfers between devices, body(): kv[offset - 1] = lax.ppermute(kv[offset - 1], 'head', to)  10.3 us
    all_gather x1, blocking collectives, body(): lax.all_gather(add_residual(parts, residual), 'head', axis_index_groups=p...  6.78 us
    ppermute x3, waiting for transfers between devices, body(): kv[offset - 1] = lax.ppermute(kv[offset - 1], 'head', to)  5.91 us
    pallas_call x1, Pallas kernels, attend_and_pick(): pl.pallas_call(attend_kernel, out_shape=(jax.ShapeDtypeStruct((ROWS, HEAD...  3.78 us
    all_to_all x1, starting transfers between devices, exchange(): lax.all_to_all(blocks, 'head', 0, 0, axis_index_groups=groups, tiled=True)  3.51 us
    unnamed x14, local copies, waits for them, and re-layouts  1.91 us
    pallas_call x1, Pallas kernels, normalize(): pl.pallas_call(norm_kernel, out_shape=(jax.ShapeDtypeStruct((ROWS, 2, OUT...  1.43 us
  transfers between devices with their start and end apart: 4, of which 2 were waited for; matrix products, arithmetic and copies ran while one was open for 0% of the time, Pallas kernels for 0%

profile of v2, /device:TPU:1, one launch (start us, length us, event | category | flops | bytes accessed | tf_op | source)
XLA Modules:
  0.0 57.3 jit_solution(3498658609072193240)
XLA Ops:
  0.6 0.0 copy-start.3
  0.6 0.0 copy-start.2
  0.7 0.0 copy-start.1
  0.7 3.8 %attend_and_pick.1 = (bf16[4,16,128]{2,1,0:T(8,128)(2,1)}, bf16[1,4,2,2,128,128]{5,4,3,2,1,0:T(8,128)(2,1)}, bf16[2,2,128,128]{3,2,1,0:T(8,128)(2,1)}, bf16[2,2,...) custom-call(s32[64]{0:T(128)} %slot_ref.1, s32[4]{0:T(128)} %len_ref.1, bf16[1,2,8,128,128]{4,3,2,1,0:T(8,128)(2,1)} %cache_ref.1, ...), custom_call_target="tpu_custom_call" | custom-call | tf_op jit(solution)/shard_map/attend_and_pick/pallas_call | solution.py:118
  4.5 9.9 %all_to_all.15.att_ref = bf16[4,16,128]{2,1,0:T(8,128)(2,1)S(1)} all-to-all(bf16[4,16,128]{2,1,0:T(8,128)(2,1)} %get-tuple-element.12), channel_id=1, replica_groups={{0,8,16,24},{1,9,17,25},{2,10,18,26},{3,11,19,27},{4,12,20,28},{5,13,21..., dimensions={0} | all-to-all | bytes 32768 | tf_op jit(solution)/shard_map/all_to_all | solution.py:259
  14.3 0.0 copy-start
  14.4 1.9 %copy-done = bf16[256,6144]{1,0:T(8,128)(2,1)S(1)} copy-done((bf16[256,6144]{1,0:T(8,128)(2,1)S(1)}, bf16[256,6144]{1,0:T(8,128)(2,1)}, u32[]{:S(2)}) %copy-start) | copy-done | bytes 3145752
  16.2 0.0 copy-start.6
  16.2 0.0 copy-start.5
  16.2 0.0 copy-start.4
  16.2 0.5 project.1
  16.8 11.8 %all_to_all.16.parts_ref = bf16[16,8,384]{2,1,0:T(8,128)(2,1)S(1)} all-to-all(bf16[16,8,384]{2,1,0:T(8,128)(2,1)S(1)} %project.1), channel_id=1, replica_groups={{0,2,4,6,8,10,12,14,16,18,20,22,24,26,28,30},{1,3,5,7,9,11,13,15,17,19,..., dimensions={0} | all-to-all | bytes 196608 | tf_op jit(solution)/shard_map/all_to_all | solution.py:259
  28.5 0.0 copy-done.3
  28.5 0.1 add_residual.1
  28.6 6.8 %all-gather = f32[16,384]{1,0:T(8,128)S(1)} all-gather(f32[8,384]{1,0:T(8,128)S(1)} %add_residual.1), channel_id=2, replica_groups={{0,1},{2,3},{4,5},{6,7},{8,9},{10,11},{12,13},{14,15},{16,17},{18,19},{..., dimensions={0}, use_global_device_ids=true | all-gather | bytes 36864 | tf_op jit(solution)/shard_map/all_gather | solution.py:271
  35.4 0.7 %round_hidden.1 = (bf16[4,2,192]{2,1,0:T(2,128)(2,1)}, bf16[16,8,384]{2,1,0:T(8,128)(2,1)}) custom-call(f32[2,8,384]{2,1,0:T(8,128)S(1)} %bitcast.3), custom_call_target="tpu_custom_call" | custom-call | tf_op jit(solution)/shard_map/round_hidden/pallas_call | solution.py:199
  36.1 3.5 %all-to-all-start.2 = ((bf16[16,8,384]{2,1,0:T(8,128)(2,1)}), bf16[16,8,384]{2,1,0:T(8,128)(2,1)S(1)}, u32[]{:S(2)}, u32[]{:S(2)}) async-start(bf16[16,8,384]{2,1,0:T(8,128)(2,1)} %get-tuple-element.13), calls=%async_computation.2 | async-start | bytes 196608 | tf_op jit(solution)/shard_map/all_to_all | solution.py:259
  39.6 0.0 copy-done.6
  39.6 3.2 %collective-permute-start = (bf16[2,2,128,128]{3,2,1,0:T(8,128)(2,1)S(1)}, bf16[2,2,128,128]{3,2,1,0:T(8,128)(2,1)S(1)}, u32[]{:S(2)}, u32[]{:S(2)}) collective-permute-start(bf16[2,2,128,128]{3,2,1,0:T(8,128)(2,1)S(1)} %copy-done.6), channel_id=1, source_target_pairs={{0,8},{1,9},{2,10},{3,11},{4,12},{5,13},{6,14},{7,15},{8,16},{9,17... | collective-permute-start | bytes 393224 | tf_op jit(solution)/shard_map/ppermute | solution.py:269
  42.8 0.0 copy-done.5
  42.8 4.0 %collective-permute-start.1 = (bf16[2,2,128,128]{3,2,1,0:T(8,128)(2,1)S(1)}, bf16[2,2,128,128]{3,2,1,0:T(8,128)(2,1)S(1)}, u32[]{:S(2)}, u32[]{:S(2)}) collective-permute-start(bf16[2,2,128,128]{3,2,1,0:T(8,128)(2,1)S(1)} %copy-done.5), channel_id=1, source_target_pairs={{0,16},{1,17},{2,18},{3,19},{4,20},{5,21},{6,22},{7,23},{8,24},{9,... | collective-permute-start | bytes 393224 | tf_op jit(solution)/shard_map/ppermute | solution.py:269
  46.9 0.0 copy-done.4
  46.9 3.1 %collective-permute-start.2 = (bf16[2,2,128,128]{3,2,1,0:T(8,128)(2,1)S(1)}, bf16[2,2,128,128]{3,2,1,0:T(8,128)(2,1)S(1)}, u32[]{:S(2)}, u32[]{:S(2)}) collective-permute-start(bf16[2,2,128,128]{3,2,1,0:T(8,128)(2,1)S(1)} %copy-done.4), channel_id=1, source_target_pairs={{0,24},{1,25},{2,26},{3,27},{4,28},{5,29},{6,30},{7,31},{8,0},{9,1... | collective-permute-start | bytes 393224 | tf_op jit(solution)/shard_map/ppermute | solution.py:269
  49.9 0.0 collective-permute-done.kv1
  49.9 4.1 %collective-permute-done.1.kv2 = bf16[2,2,128,128]{3,2,1,0:T(8,128)(2,1)S(1)} collective-permute-done((bf16[2,2,128,128]{3,2,1,0:T(8,128)(2,1)S(1)}, bf16[2,2,128,128]{3,2,1,0:T(8,128)(2,1)S(1)}, u32[]{:S(2)}, u32[]{:S(2)}) %collective-permute-start.1) | collective-permute-done | bytes 131104 | tf_op jit(solution)/shard_map/ppermute | solution.py:269
  54.0 1.8 %collective-permute-done.2.kv3 = bf16[2,2,128,128]{3,2,1,0:T(8,128)(2,1)S(1)} collective-permute-done((bf16[2,2,128,128]{3,2,1,0:T(8,128)(2,1)S(1)}, bf16[2,2,128,128]{3,2,1,0:T(8,128)(2,1)S(1)}, u32[]{:S(2)}, u32[]{:S(2)}) %collective-permute-start.2) | collective-permute-done | bytes 131104 | tf_op jit(solution)/shard_map/ppermute | solution.py:269
  55.9 0.0 all-to-all-done.2.blocks_ref
  55.9 0.0 copy-done.2
  55.9 0.0 copy-done.1
  55.9 1.4 %normalize.1 = (bf16[4,2,6144]{2,1,0:T(2,128)(2,1)}, bf16[1,4,2,2,128,128]{5,4,3,2,1,0:T(8,128)(2,1)}) custom-call(bf16[16,8,384]{2,1,0:T(8,128)(2,1)S(1)} %all-to-all-done.2.blocks_ref, f32[48,128]{1,0:T(8,128)S(1)} %bitcast.4, f32[48,128]{1,0:T(8,128)S(1)} %bitcast.5, ...), custom_call_target="tpu_custom_call", output_to_operand_aliasing={{1}: (6, {})} | custom-call | tf_op jit(solution)/shard_map/normalize/pallas_call | solution.py:243
Async XLA Ops:
  0.6 27.9 %copy-start.3 = (bf16[4,2,192]{2,1,0:T(2,128)(2,1)S(1)}, bf16[4,2,192]{2,1,0:T(2,128)(2,1)}, u32[]{:S(2)}) copy-start(bf16[4,2,192]{2,1,0:T(2,128)(2,1)} %residual_ref.1) | copy-start | bytes 9220
  0.6 55.2 %copy-start.2 = (f32[6144]{0:T(1024)S(1)}, f32[6144]{0:T(1024)}, u32[]{:S(2)}) copy-start(f32[6144]{0:T(1024)} %param.15) | copy-start | bytes 73732
  0.7 55.2 %copy-start.1 = (f32[6144]{0:T(1024)S(1)}, f32[6144]{0:T(1024)}, u32[]{:S(2)}) copy-start(f32[6144]{0:T(1024)} %param.14) | copy-start | bytes 73732
  14.3 1.9 %copy-start = (bf16[256,6144]{1,0:T(8,128)(2,1)S(1)}, bf16[256,6144]{1,0:T(8,128)(2,1)}, u32[]{:S(2)}) copy-start(bf16[256,6144]{1,0:T(8,128)(2,1)} %weight_ref.1) | copy-start | bytes 9437188
  16.2 23.4 %copy-start.6 = (bf16[2,2,128,128]{3,2,1,0:T(8,128)(2,1)S(1)}, bf16[2,2,128,128]{3,2,1,0:T(8,128)(2,1)}, u32[]{:S(2)}) copy-start(bf16[2,2,128,128]{3,2,1,0:T(8,128)(2,1)} %get-tuple-element.14) | copy-start | bytes 393220
  16.2 26.5 %copy-start.5 = (bf16[2,2,128,128]{3,2,1,0:T(8,128)(2,1)S(1)}, bf16[2,2,128,128]{3,2,1,0:T(8,128)(2,1)}, u32[]{:S(2)}) copy-start(bf16[2,2,128,128]{3,2,1,0:T(8,128)(2,1)} %get-tuple-element.15) | copy-start | bytes 393220
  16.2 30.6 %copy-start.4 = (bf16[2,2,128,128]{3,2,1,0:T(8,128)(2,1)S(1)}, bf16[2,2,128,128]{3,2,1,0:T(8,128)(2,1)}, u32[]{:S(2)}) copy-start(bf16[2,2,128,128]{3,2,1,0:T(8,128)(2,1)} %get-tuple-element.16) | copy-start | bytes 393220
  36.1 19.8 %all-to-all-start.2 = ((bf16[16,8,384]{2,1,0:T(8,128)(2,1)}), bf16[16,8,384]{2,1,0:T(8,128)(2,1)S(1)}, u32[]{:S(2)}, u32[]{:S(2)}) async-start(bf16[16,8,384]{2,1,0:T(8,128)(2,1)} %get-tuple-element.13), calls=%async_computation.2 | async-start | bytes 196608 | tf_op jit(solution)/shard_map/all_to_all | solution.py:259
  39.6 10.3 %collective-permute-start = (bf16[2,2,128,128]{3,2,1,0:T(8,128)(2,1)S(1)}, bf16[2,2,128,128]{3,2,1,0:T(8,128)(2,1)S(1)}, u32[]{:S(2)}, u32[]{:S(2)}) collective-permute-start(bf16[2,2,128,128]{3,2,1,0:T(8,128)(2,1)S(1)} %copy-done.6), channel_id=1, source_target_pairs={{0,8},{1,9},{2,10},{3,11},{4,12},{5,13},{6,14},{7,15},{8,16},{9,17... | collective-permute-start | bytes 393224 | tf_op jit(solution)/shard_map/ppermute | solution.py:269
  42.8 11.2 %collective-permute-start.1 = (bf16[2,2,128,128]{3,2,1,0:T(8,128)(2,1)S(1)}, bf16[2,2,128,128]{3,2,1,0:T(8,128)(2,1)S(1)}, u32[]{:S(2)}, u32[]{:S(2)}) collective-permute-start(bf16[2,2,128,128]{3,2,1,0:T(8,128)(2,1)S(1)} %copy-done.5), channel_id=1, source_target_pairs={{0,16},{1,17},{2,18},{3,19},{4,20},{5,21},{6,22},{7,23},{8,24},{9,... | collective-permute-start | bytes 393224 | tf_op jit(solution)/shard_map/ppermute | solution.py:269
  46.9 9.0 %collective-permute-start.2 = (bf16[2,2,128,128]{3,2,1,0:T(8,128)(2,1)S(1)}, bf16[2,2,128,128]{3,2,1,0:T(8,128)(2,1)S(1)}, u32[]{:S(2)}, u32[]{:S(2)}) collective-permute-start(bf16[2,2,128,128]{3,2,1,0:T(8,128)(2,1)S(1)} %copy-done.4), channel_id=1, source_target_pairs={{0,24},{1,25},{2,26},{3,27},{4,28},{5,29},{6,30},{7,31},{8,0},{9,1... | collective-permute-start | bytes 393224 | tf_op jit(solution)/shard_map/ppermute | solution.py:269

commit v3 on v2

--- a/solution.py
+++ b/solution.py
@@ -28,15 +28,28 @@
 ANY = pl.BlockSpec(memory_space=pl.ANY)
 
 
+def estimate(microseconds):
+    return pl.CostEstimate(
+        flops=0, transcendentals=0, bytes_accessed=int(microseconds * 3.69e6)
+    )
+
+
 def attend_kernel(
-    slot_ref, len_ref, cache_ref, fresh_ref, att_ref, new_ref, kv1, kv2, kv3, held, att_scr, in_sems, sems
+    slot_hbm, len_hbm, cache_ref, fresh_hbm, att_ref, new_ref, kv1, kv2, kv3,
+    slot_scr, len_scr, fresh_scr, held, att_scr, in_sems, sems,
 ):
     me = lax.axis_index("head")
     row = me // OLD
     lane = me % OLD
     loads = []
-    for kind in range(2):
-        load = pltpu.make_async_copy(cache_ref.at[0, kind], held.at[kind], in_sems.at[kind])
+    for source, target in (
+        (cache_ref.at[0, 0], held.at[0]),
+        (fresh_hbm, fresh_scr),
+        (slot_hbm, slot_scr),
+        (len_hbm, len_scr),
+        (cache_ref.at[0, 1], held.at[1]),
+    ):
+        load = pltpu.make_async_copy(source, target, in_sems.at[len(loads)])
         load.start()
         loads.append(load)
     copies = []
@@ -45,18 +58,18 @@
         for offset, kv_ref in ((1, kv1), (2, kv2), (3, kv3), (0, new_ref.at[0, row])):
             target = (row + offset) % ROWS
             for i in range(HEAD_DEV):
-                slot = slot_ref[(target * OLD + lane) * HEAD_DEV + i]
+                slot = slot_scr[(target * OLD + lane) * HEAD_DEV + i]
                 copy = pltpu.make_async_copy(
                     held.at[kind, slot], kv_ref.at[kind, i], sems.at[len(copies)]
                 )
                 copy.start()
                 copies.append(copy)
 
-    length = len_ref[row]
     scale = 1.0 / math.sqrt(HEAD_DIM)
     query_rows, old_scores, new_first, new_second = [], [], [], []
     odd = lax.broadcasted_iota(jnp.int32, (8, HEAD_DIM), 0) % 2 == 1
-    fresh = fresh_ref[0].astype(F32)
+    loads[1].wait()
+    fresh = fresh_scr[0].astype(F32)
     for slot in range(SLOTS):
         query = jnp.where(
             odd,
@@ -67,6 +80,7 @@
         new_first.append(jnp.sum(query * fresh[1, 0, slot : slot + 1], axis=-1, keepdims=True))
         new_second.append(jnp.sum(query * fresh[1, 1, slot : slot + 1], axis=-1, keepdims=True))
     loads[0].wait()
+    loads[2].wait()
     pick(0)
     for slot in range(SLOTS):
         old_scores.append(
@@ -81,7 +95,8 @@
     scores = jnp.concatenate(old_scores, axis=0) * scale
     first = jnp.concatenate(new_first, axis=0) * scale
     second = jnp.concatenate(new_second, axis=0) * scale
-    visible = lax.broadcasted_iota(jnp.int32, shape, 1) < length
+    loads[3].wait()
+    visible = lax.broadcasted_iota(jnp.int32, shape, 1) < len_scr[row]
     later = lax.broadcasted_iota(jnp.int32, (SLOTS * 8, 1), 0) % 2 == 1
     scores = jnp.where(visible, scores, -1e30)
     second = jnp.where(later, second, -1e30)
@@ -94,7 +109,7 @@
     first_w = (first_exp / total).astype(BF16).astype(F32)
     second_w = (second_exp / total).astype(BF16).astype(F32)
     mine = lax.broadcasted_iota(jnp.int32, (8, HEAD_DIM), 0) // 2 == row
-    loads[1].wait()
+    loads[4].wait()
     pick(1)
     for slot in range(SLOTS):
         part = slice(slot * 8, slot * 8 + 8)
@@ -106,7 +121,7 @@
         att_scr[slot] = jnp.where(mine, result, 0.0)
     for target in range(ROWS):
         pair = [
-            att_scr[slot_ref[(target * OLD + lane) * HEAD_DEV + i]] for i in range(HEAD_DEV)
+            att_scr[slot_scr[(target * OLD + lane) * HEAD_DEV + i]] for i in range(HEAD_DEV)
         ]
         att_ref[target] = jnp.concatenate(pair, axis=0).astype(BF16)
     for copy in copies:
@@ -122,20 +137,41 @@
             jax.ShapeDtypeStruct((1, ROWS) + block, BF16),
             *[jax.ShapeDtypeStruct(block, BF16)] * (ROWS - 1),
         ),
-        in_specs=[SMEM, SMEM, ANY, VMEM],
+        in_specs=[ANY] * 4,
         out_specs=(VMEM, *[ANY] * ROWS),
         scratch_shapes=[
+            pltpu.SMEM(slot_map.shape, jnp.int32),
+            pltpu.SMEM(lengths.shape, jnp.int32),
+            pltpu.VMEM(fresh.shape, BF16),
             pltpu.VMEM((2, SLOTS, LEN, HEAD_DIM), BF16),
             pltpu.VMEM((SLOTS, 8, HEAD_DIM), F32),
-            pltpu.SemaphoreType.DMA((2,)),
+            pltpu.SemaphoreType.DMA((5,)),
             pltpu.SemaphoreType.DMA((ROWS * HEAD_DEV * 2,)),
         ],
+        cost_estimate=estimate(3.5),
         compiler_params=pltpu.CompilerParams(vmem_limit_bytes=FIRST_LIMIT),
         name="attend_and_pick",
     )(slot_map, lengths, cache, fresh)
 
 
-def project_kernel(att_ref, weight_ref, out_ref):
+def touch_kernel(weight_ref, out_ref):
+    out_ref[...] = weight_ref[:16, :128]
+
+
+def touch(out_weight):
+    return pl.pallas_call(
+        touch_kernel,
+        out_shape=jax.ShapeDtypeStruct((16, 128), BF16),
+        in_specs=[VMEM],
+        out_specs=VMEM,
+        cost_estimate=estimate(0.2),
+        compiler_params=pltpu.CompilerParams(vmem_limit_bytes=VMEM_LIMIT),
+        name="touch",
+    )(out_weight)
+
+
+def project_kernel(att_ref, weight_ref, *refs):
+    out_ref = refs[-1]
     total = att_ref[0].astype(F32)
     for row in range(1, ROWS):
         total = total + att_ref[row].astype(F32)
@@ -149,18 +185,20 @@
         out_ref[chip] = part.astype(BF16)
 
 
-def project(attended, out_weight):
+def project(attended, out_weight, *arrived):
     return pl.pallas_call(
         project_kernel,
         out_shape=jax.ShapeDtypeStruct((CHIPS, 8, CHUNK), BF16),
-        in_specs=[VMEM, VMEM],
+        in_specs=[VMEM, VMEM] + [ANY] * len(arrived),
         out_specs=VMEM,
+        cost_estimate=estimate(0.6),
         compiler_params=pltpu.CompilerParams(vmem_limit_bytes=VMEM_LIMIT),
         name="project",
-    )(attended, out_weight)
-
-
-def add_kernel(parts_ref, residual_ref, out_ref):
+    )(attended, out_weight, *arrived)
+
+
+def add_kernel(parts_ref, residual_ref, *refs):
+    out_ref = refs[-1]
     core = lax.axis_index("head") % CORES
     total = parts_ref[0].astype(F32)
     for chip in range(1, CHIPS):
@@ -173,18 +211,20 @@
     out_ref[...] = total + own
 
 
-def add_residual(parts, residual):
+def add_residual(parts, residual, *arrived):
     return pl.pallas_call(
         add_kernel,
         out_shape=jax.ShapeDtypeStruct((8, CHUNK), F32),
-        in_specs=[VMEM, VMEM],
+        in_specs=[VMEM, VMEM] + [ANY] * len(arrived),
         out_specs=VMEM,
+        cost_estimate=estimate(0.2),
         compiler_params=pltpu.CompilerParams(vmem_limit_bytes=VMEM_LIMIT),
         name="add_residual",
-    )(parts, residual)
-
-
-def hidden_kernel(sums_ref, hidden_ref, spread_ref):
+    )(parts, residual, *arrived)
+
+
+def hidden_kernel(sums_ref, *refs):
+    hidden_ref, spread_ref = refs[-2:]
     core = lax.axis_index("head") % CORES
     total = sums_ref[0] + sums_ref[1]
     hidden = total.astype(BF16)
@@ -195,18 +235,19 @@
         spread_ref[chip] = hidden
 
 
-def round_hidden(sums):
+def round_hidden(sums, *arrived):
     return pl.pallas_call(
         hidden_kernel,
         out_shape=(
             jax.ShapeDtypeStruct((ROWS, 2, SHARE), BF16),
             jax.ShapeDtypeStruct((CHIPS, 8, CHUNK), BF16),
         ),
-        in_specs=[VMEM],
+        in_specs=[VMEM] + [ANY] * len(arrived),
         out_specs=(VMEM, VMEM),
+        cost_estimate=estimate(0.6),
         compiler_params=pltpu.CompilerParams(vmem_limit_bytes=VMEM_LIMIT),
         name="round_hidden",
-    )(sums)
+    )(sums, *arrived)
 
 
 def norm_kernel(blocks_ref, gain_ref, bias_ref, kv1, kv2, kv3, _, out_ref, cache_ref, sems):
@@ -250,6 +291,7 @@
         out_specs=(VMEM, ANY),
         scratch_shapes=[pltpu.SemaphoreType.DMA((ROWS - 1,))],
         input_output_aliases={6: 1},
+        cost_estimate=estimate(1.4),
         compiler_params=pltpu.CompilerParams(vmem_limit_bytes=VMEM_LIMIT),
         name="normalize",
     )(blocks, gain.reshape(OUT // 128, 128), bias.reshape(OUT // 128, 128), *kv, cache_new)
@@ -267,10 +309,15 @@
     for offset in range(1, ROWS):
         to = [(i, (i + offset * OLD) % MEMBERS) for i in range(MEMBERS)]
         kv[offset - 1] = lax.ppermute(kv[offset - 1], "head", to)
-    parts = exchange(project(exchange(picked, columns), out_weight), sides)
-    sums = lax.all_gather(add_residual(parts, residual), "head", axis_index_groups=pairs)
-    hidden, copies = round_hidden(sums)
-    normed, cache_new = normalize(exchange(copies, sides), norm_gain, norm_bias, kv, cache_new)
+    parts = exchange(project(exchange(picked, columns), out_weight, touch(out_weight)), sides)
+
+    def finish(blocks, hidden):
+        sums = lax.all_gather(add_residual(blocks, hidden), "head", axis_index_groups=pairs)
+        hidden, copies = round_hidden(sums)
+        return exchange(copies, sides), hidden
+
+    blocks, hidden = lax.cond(lax.axis_index("head") < MEMBERS, finish, lambda a, b: (a, b), parts, residual)
+    normed, cache_new = normalize(blocks, norm_gain, norm_bias, kv, cache_new)
     return (cache_new, hidden, normed)
 
 

time: 57.8 us -> 50.5 us (0.87)
  blocking collectives: 28.5 us -> 16.9 us
  starting transfers between devices: 13.8 us -> 22.2 us
  waiting for transfers between devices: 5.91 us -> 2.54 us
  Pallas kernels: 6.49 us -> 5.83 us
    all_to_all x2 -> x1, blocking collectives: 21.7 us -> 11.4 us  [exchange(): lax.all_to_all(blocks, 'head', 0, 0, axis_index_groups=groups, tiled=True)]
    all_to_all x1 -> x2, starting transfers between devices: 3.51 us -> 11.8 us  [exchange(): lax.all_to_all(blocks, 'head', 0, 0, axis_index_groups=groups, tiled=True)]
    ppermute x3, waiting for transfers between devices: 5.91 us -> 0.01 us  [body(): kv[offset - 1] = lax.ppermute(kv[offset - 1], 'head', to)]
    all_to_all x1 -> x2, waiting for transfers between devices: 0.01 us -> 2.53 us  [exchange(): lax.all_to_all(blocks, 'head', 0, 0, axis_index_groups=groups, tiled=True)]
    all_gather x1, blocking collectives: 6.78 us -> 5.45 us  [finish(): lax.all_gather(add_residual(blocks, hidden), 'head', axis_index_groups=pa...]
    pallas_call x1, Pallas kernels: 3.78 us -> 3.04 us  [attend_and_pick(): pl.pallas_call(attend_kernel, out_shape=(jax.ShapeDtypeStruct((ROWS, HEAD...]
    pallas_call x1, Pallas kernels: 0.51 us -> 1.17 us  [project(): pl.pallas_call(project_kernel, out_shape=jax.ShapeDtypeStruct((CHIPS, 8,...]
    pallas_call x1, Pallas kernels: 0.67 us -> 0.08 us  [round_hidden(): pl.pallas_call(hidden_kernel, out_shape=(jax.ShapeDtypeStruct((ROWS, 2, S...]
  transfers between devices with their start and end apart: 4 -> 5, of which waited for: 2 -> 1; matrix products, arithmetic and copies ran while one was open for 0% -> 0% of each run, Pallas kernels for 0% -> 0%
where the time goes in v3:
time: 50.5 us; the launch traced here: 50.1 us
  starting transfers between devices  22.2 us (44%)
  blocking collectives  16.9 us (33%)
  Pallas kernels  5.83 us (12%)
  waiting for transfers between devices  2.54 us (5%)
  local copies, waits for them, and re-layouts  1.92 us (4%)
  between operations  0.77 us (2%)
    all_to_all x2, starting transfers between devices, exchange(): lax.all_to_all(blocks, 'head', 0, 0, axis_index_groups=groups, tiled=True)  11.8 us
    all_to_all x1, blocking collectives, exchange(): lax.all_to_all(blocks, 'head', 0, 0, axis_index_groups=groups, tiled=True)  11.4 us
    ppermute x3, starting transfers between devices, body(): kv[offset - 1] = lax.ppermute(kv[offset - 1], 'head', to)  10.3 us
    all_gather x1, blocking collectives, finish(): lax.all_gather(add_residual(blocks, hidden), 'head', axis_index_groups=pa...  5.45 us
    pallas_call x1, Pallas kernels, attend_and_pick(): pl.pallas_call(attend_kernel, out_shape=(jax.ShapeDtypeStruct((ROWS, HEAD...  3.04 us
    all_to_all x2, waiting for transfers between devices, exchange(): lax.all_to_all(blocks, 'head', 0, 0, axis_index_groups=groups, tiled=True)  2.53 us
    unnamed x16, local copies, waits for them, and re-layouts  1.92 us
    pallas_call x1, Pallas kernels, normalize(): pl.pallas_call(norm_kernel, out_shape=(jax.ShapeDtypeStruct((ROWS, 2, OUT...  1.45 us
  transfers between devices with their start and end apart: 5, of which 1 were waited for; matrix products, arithmetic and copies ran while one was open for 0% of the time, Pallas kernels for 0%

profile of v3, /device:TPU:1, one launch (start us, length us, event | category | flops | bytes accessed | tf_op | source)
XLA Modules:
  0.0 50.1 jit_solution(17526783391548595663)
XLA Ops:
  0.6 3.0 %attend_and_pick.1 = (bf16[4,16,128]{2,1,0:T(8,128)(2,1)}, bf16[1,4,2,2,128,128]{5,4,3,2,1,0:T(8,128)(2,1)}, bf16[2,2,128,128]{3,2,1,0:T(8,128)(2,1)}, bf16[2,2,...) custom-call(s32[64]{0:T(128)} %slot_hbm.1, s32[4]{0:T(128)} %len_hbm.1, bf16[1,2,8,128,128]{4,3,2,1,0:T(8,128)(2,1)} %cache_ref.1, ...), custom_call_target="tpu_custom_call" | custom-call | bytes 12915000 | tf_op jit(solution)/shard_map/attend_and_pick/pallas_call | solution.py:133
  3.7 5.4 %all-to-all-start.1 = ((bf16[4,16,128]{2,1,0:T(8,128)(2,1)}), bf16[4,16,128]{2,1,0:T(8,128)(2,1)S(1)}, u32[]{:S(2)}, u32[]{:S(2)}) async-start(bf16[4,16,128]{2,1,0:T(8,128)(2,1)} %get-tuple-element.24), calls=%async_computation.1 | async-start | bytes 32768 | tf_op jit(solution)/shard_map/all_to_all | solution.py:301
  9.1 0.0 copy-start
  9.1 1.9 %copy-done = bf16[256,6144]{1,0:T(8,128)(2,1)S(1)} copy-done((bf16[256,6144]{1,0:T(8,128)(2,1)S(1)}, bf16[256,6144]{1,0:T(8,128)(2,1)}, u32[]{:S(2)}) %copy-start) | copy-done | bytes 3145752
  11.0 0.0 copy-start.1
  11.0 0.0 copy-start.7
  11.0 0.0 copy-start.6
  11.0 0.0 copy-start.5
  11.0 0.0 copy-start.2
  11.0 0.0 copy-start.3
  11.0 2.5 %all-to-all-done.1.att_ref = bf16[4,16,128]{2,1,0:T(8,128)(2,1)S(1)} async-done(((bf16[4,16,128]{2,1,0:T(8,128)(2,1)}), bf16[4,16,128]{2,1,0:T(8,128)(2,1)S(1)}, u32[]{:S(2)}, u32[]{:S(2)}) %all-to-all-start.1) | async-done | bytes 16416 | tf_op jit(solution)/shard_map/all_to_all | solution.py:301
  13.6 0.0 copy-done.1
  13.6 1.2 %project.1 = bf16[16,8,384]{2,1,0:T(8,128)(2,1)} custom-call(bf16[4,16,128]{2,1,0:T(8,128)(2,1)S(1)} %all-to-all-done.1.att_ref, bf16[256,6144]{1,0:T(8,128)(2,1)S(1)} %copy-done.1, bf16[16,128]{1,0:T(8,128)(2,1)S(1)} %touch.1.refs_0_), custom_call_target="tpu_custom_call" | custom-call | bytes 2214000 | tf_op jit(solution)/shard_map/project/pallas_call | solution.py:189
  14.7 6.4 %all-to-all-start.2 = ((bf16[16,8,384]{2,1,0:T(8,128)(2,1)}), bf16[16,8,384]{2,1,0:T(8,128)(2,1)S(1)}, u32[]{:S(2)}, u32[]{:S(2)}) async-start(bf16[16,8,384]{2,1,0:T(8,128)(2,1)} %project.1), calls=%async_computation.2 | async-start | bytes 196608 | tf_op jit(solution)/shard_map/all_to_all | solution.py:301
  21.2 3.3 %collective-permute-start = (bf16[2,2,128,128]{3,2,1,0:T(8,128)(2,1)}, bf16[2,2,128,128]{3,2,1,0:T(8,128)(2,1)S(1)}, u32[]{:S(2)}, u32[]{:S(2)}) collective-permute-start(bf16[2,2,128,128]{3,2,1,0:T(8,128)(2,1)} %get-tuple-element.26), channel_id=1, source_target_pairs={{0,8},{1,9},{2,10},{3,11},{4,12},{5,13},{6,14},{7,15},{8,16},{9,17... | collective-permute-start | bytes 393224 | tf_op jit(solution)/shard_map/ppermute | solution.py:311
  24.4 0.0 copy-done.7
  24.5 4.0 %collective-permute-start.1 = (bf16[2,2,128,128]{3,2,1,0:T(8,128)(2,1)S(1)}, bf16[2,2,128,128]{3,2,1,0:T(8,128)(2,1)S(1)}, u32[]{:S(2)}, u32[]{:S(2)}) collective-permute-start(bf16[2,2,128,128]{3,2,1,0:T(8,128)(2,1)S(1)} %copy-done.7), channel_id=1, source_target_pairs={{0,16},{1,17},{2,18},{3,19},{4,20},{5,21},{6,22},{7,23},{8,24},{9,... | collective-permute-start | bytes 393224 | tf_op jit(solution)/shard_map/ppermute | solution.py:311
  28.5 0.0 copy-done.6
  28.5 3.1 %collective-permute-start.2 = (bf16[2,2,128,128]{3,2,1,0:T(8,128)(2,1)S(1)}, bf16[2,2,128,128]{3,2,1,0:T(8,128)(2,1)S(1)}, u32[]{:S(2)}, u32[]{:S(2)}) collective-permute-start(bf16[2,2,128,128]{3,2,1,0:T(8,128)(2,1)S(1)} %copy-done.6), channel_id=1, source_target_pairs={{0,24},{1,25},{2,26},{3,27},{4,28},{5,29},{6,30},{7,31},{8,0},{9,1... | collective-permute-start | bytes 393224 | tf_op jit(solution)/shard_map/ppermute | solution.py:311
  31.6 0.0 all-to-all-done.2
  31.6 0.0 copy-done.5
  31.6 17.0 %conditional.1 = ((bf16[16,8,384]{2,1,0:T(8,128)(2,1)S(1)}, bf16[4,2,192]{2,1,0:T(2,128)(2,1)S(1)})) conditional(s32[]{:T(128)} %convert_element_type.3, (bf16[16,8,384]{2,1,0:T(8,128)(2,1)S(1)}, bf16[4,2,192]{2,1,0:T(2,128)(2,1)S(1)}) %tuple.21, (bf16[16,8,384]{2,1,0:T(8,128)(2,1)S(1)}, bf16[4,2,192]{2,1,0:T(2,128)(2,1)S(1)}) %tuple.22), branch_computations={%region_0.0_spmd, %region_1.0_spmd} | conditional | bytes 3185496 | solution.py:319
  31.6 0.1 add_residual.1
  31.7 5.5 %all-gather = f32[16,384]{1,0:T(8,128)S(1)} all-gather(f32[8,384]{1,0:T(8,128)S(1)} %add_residual.1), channel_id=2, replica_groups={{0,1},{2,3},{4,5},{6,7},{8,9},{10,11},{12,13},{14,15},{16,17},{18,19},{..., dimensions={0}, use_global_device_ids=true | all-gather | bytes 36864 | tf_op jit(solution)/shard_map/cond/branch_1_fun/all_gather | solution.py:315
  37.1 0.1 round_hidden.1
  37.2 11.4 %all_to_all.14 = bf16[16,8,384]{2,1,0:T(8,128)(2,1)S(1)} all-to-all(bf16[16,8,384]{2,1,0:T(8,128)(2,1)S(1)} %get-tuple-element.10), channel_id=1, replica_groups={{0,2,4,6,8,10,12,14,16,18,20,22,24,26,28,30},{1,3,5,7,9,11,13,15,17,19,..., dimensions={0} | all-to-all | bytes 196608 | tf_op jit(solution)/shard_map/cond/branch_1_fun/all_to_all | solution.py:301
  48.6 0.0 copy-start.4
  48.6 0.0 collective-permute-done.kv1
  48.6 0.0 collective-permute-done.1.kv2
  48.6 0.0 collective-permute-done.2.kv3
  48.6 0.0 copy-done.2
  48.7 0.0 copy-done.3
  48.7 1.5 %normalize.1 = (bf16[4,2,6144]{2,1,0:T(2,128)(2,1)}, bf16[1,4,2,2,128,128]{5,4,3,2,1,0:T(8,128)(2,1)}) custom-call(bf16[16,8,384]{2,1,0:T(8,128)(2,1)S(1)} %get-tuple-element.25.blocks_ref, f32[48,128]{1,0:T(8,128)S(1)} %bitcast.4, f32[48,128]{1,0:T(8,128)S(1)} %bitcast.5, ...), custom_call_target="tpu_custom_call", output_to_operand_aliasing={{1}: (6, {})} | custom-call | bytes 5166000 | tf_op jit(solution)/shard_map/normalize/pallas_call | solution.py:284
  50.1 0.0 copy-done.4
  (1 shorter events, 0.0 us)
Async XLA Ops:
  3.7 9.9 %all-to-all-start.1 = ((bf16[4,16,128]{2,1,0:T(8,128)(2,1)}), bf16[4,16,128]{2,1,0:T(8,128)(2,1)S(1)}, u32[]{:S(2)}, u32[]{:S(2)}) async-start(bf16[4,16,128]{2,1,0:T(8,128)(2,1)} %get-tuple-element.24), calls=%async_computation.1 | async-start | bytes 32768 | tf_op jit(solution)/shard_map/all_to_all | solution.py:301
  9.1 1.9 %copy-start = (bf16[256,6144]{1,0:T(8,128)(2,1)S(1)}, bf16[256,6144]{1,0:T(8,128)(2,1)}, u32[]{:S(2)}) copy-start(bf16[256,6144]{1,0:T(8,128)(2,1)} %weight_ref.3) | copy-start | bytes 9437188
  11.0 2.6 %copy-start.1 = (bf16[256,6144]{1,0:T(8,128)(2,1)S(1)}, bf16[256,6144]{1,0:T(8,128)(2,1)}, u32[]{:S(2)}) copy-start(bf16[256,6144]{1,0:T(8,128)(2,1)} %weight_ref.3) | copy-start | bytes 9437188
  11.0 13.4 %copy-start.7 = (bf16[2,2,128,128]{3,2,1,0:T(8,128)(2,1)S(1)}, bf16[2,2,128,128]{3,2,1,0:T(8,128)(2,1)}, u32[]{:S(2)}) copy-start(bf16[2,2,128,128]{3,2,1,0:T(8,128)(2,1)} %get-tuple-element.27) | copy-start | bytes 393220
  11.0 17.4 %copy-start.6 = (bf16[2,2,128,128]{3,2,1,0:T(8,128)(2,1)S(1)}, bf16[2,2,128,128]{3,2,1,0:T(8,128)(2,1)}, u32[]{:S(2)}) copy-start(bf16[2,2,128,128]{3,2,1,0:T(8,128)(2,1)} %get-tuple-element.28) | copy-start | bytes 393220
  11.0 20.6 %copy-start.5 = (bf16[4,2,192]{2,1,0:T(2,128)(2,1)S(1)}, bf16[4,2,192]{2,1,0:T(2,128)(2,1)}, u32[]{:S(2)}) copy-start(bf16[4,2,192]{2,1,0:T(2,128)(2,1)} %param.15) | copy-start | bytes 9220
  11.0 37.6 %copy-start.2 = (f32[6144]{0:T(1024)S(1)}, f32[6144]{0:T(1024)}, u32[]{:S(2)}) copy-start(f32[6144]{0:T(1024)} %param.16) | copy-start | bytes 73732
  11.0 37.6 %copy-start.3 = (f32[6144]{0:T(1024)S(1)}, f32[6144]{0:T(1024)}, u32[]{:S(2)}) copy-start(f32[6144]{0:T(1024)} %param.17) | copy-start | bytes 73732
  14.7 16.8 %all-to-all-start.2 = ((bf16[16,8,384]{2,1,0:T(8,128)(2,1)}), bf16[16,8,384]{2,1,0:T(8,128)(2,1)S(1)}, u32[]{:S(2)}, u32[]{:S(2)}) async-start(bf16[16,8,384]{2,1,0:T(8,128)(2,1)} %project.1), calls=%async_computation.2 | async-start | bytes 196608 | tf_op jit(solution)/shard_map/all_to_all | solution.py:301
  21.2 27.5 %collective-permute-start = (bf16[2,2,128,128]{3,2,1,0:T(8,128)(2,1)}, bf16[2,2,128,128]{3,2,1,0:T(8,128)(2,1)S(1)}, u32[]{:S(2)}, u32[]{:S(2)}) collective-permute-start(bf16[2,2,128,128]{3,2,1,0:T(8,128)(2,1)} %get-tuple-element.26), channel_id=1, source_target_pairs={{0,8},{1,9},{2,10},{3,11},{4,12},{5,13},{6,14},{7,15},{8,16},{9,17... | collective-permute-start | bytes 393224 | tf_op jit(solution)/shard_map/ppermute | solution.py:311
  24.5 24.2 %collective-permute-start.1 = (bf16[2,2,128,128]{3,2,1,0:T(8,128)(2,1)S(1)}, bf16[2,2,128,128]{3,2,1,0:T(8,128)(2,1)S(1)}, u32[]{:S(2)}, u32[]{:S(2)}) collective-permute-start(bf16[2,2,128,128]{3,2,1,0:T(8,128)(2,1)S(1)} %copy-done.7), channel_id=1, source_target_pairs={{0,16},{1,17},{2,18},{3,19},{4,20},{5,21},{6,22},{7,23},{8,24},{9,... | collective-permute-start | bytes 393224 | tf_op jit(solution)/shard_map/ppermute | solution.py:311
  28.5 20.2 %collective-permute-start.2 = (bf16[2,2,128,128]{3,2,1,0:T(8,128)(2,1)S(1)}, bf16[2,2,128,128]{3,2,1,0:T(8,128)(2,1)S(1)}, u32[]{:S(2)}, u32[]{:S(2)}) collective-permute-start(bf16[2,2,128,128]{3,2,1,0:T(8,128)(2,1)S(1)} %copy-done.6), channel_id=1, source_target_pairs={{0,24},{1,25},{2,26},{3,27},{4,28},{5,29},{6,30},{7,31},{8,0},{9,1... | collective-permute-start | bytes 393224 | tf_op jit(solution)/shard_map/ppermute | solution.py:311
  48.6 1.5 %copy-start.4 = (bf16[4,2,192]{2,1,0:T(2,128)(2,1)}, bf16[4,2,192]{2,1,0:T(2,128)(2,1)S(1)}, u32[]{:S(2)}) copy-start(bf16[4,2,192]{2,1,0:T(2,128)(2,1)S(1)} %get-tuple-element.22) | copy-start | bytes 9220

commit v4 on v3

--- a/solution.py
+++ b/solution.py
@@ -1,3 +1,4 @@
+import functools
 import math
 
 import jax
@@ -26,6 +27,7 @@
 SMEM = pl.BlockSpec(memory_space=pltpu.SMEM)
 VMEM = pl.BlockSpec(memory_space=pltpu.VMEM)
 ANY = pl.BlockSpec(memory_space=pl.ANY)
+HBM = pl.BlockSpec(memory_space=pltpu.HBM)
 
 
 def estimate(microseconds):
@@ -35,7 +37,7 @@
 
 
 def attend_kernel(
-    slot_hbm, len_hbm, cache_ref, fresh_hbm, att_ref, new_ref, kv1, kv2, kv3,
+    slot_hbm, len_hbm, cache_ref, fresh_hbm, att_ref, kv0, kv1, kv2, kv3,
     slot_scr, len_scr, fresh_scr, held, att_scr, in_sems, sems,
 ):
     me = lax.axis_index("head")
@@ -55,7 +57,7 @@
     copies = []
 
     def pick(kind):
-        for offset, kv_ref in ((1, kv1), (2, kv2), (3, kv3), (0, new_ref.at[0, row])):
+        for offset, kv_ref in ((1, kv1), (2, kv2), (3, kv3), (0, kv0)):
             target = (row + offset) % ROWS
             for i in range(HEAD_DEV):
                 slot = slot_scr[(target * OLD + lane) * HEAD_DEV + i]
@@ -91,6 +93,8 @@
                 preferred_element_type=F32,
             )
         )
+    loads[4].wait()
+    pick(1)
     shape = (SLOTS * 8, LEN)
     scores = jnp.concatenate(old_scores, axis=0) * scale
     first = jnp.concatenate(new_first, axis=0) * scale
@@ -109,8 +113,6 @@
     first_w = (first_exp / total).astype(BF16).astype(F32)
     second_w = (second_exp / total).astype(BF16).astype(F32)
     mine = lax.broadcasted_iota(jnp.int32, (8, HEAD_DIM), 0) // 2 == row
-    loads[4].wait()
-    pick(1)
     for slot in range(SLOTS):
         part = slice(slot * 8, slot * 8 + 8)
         result = jnp.dot(old_w[part], held[1, slot], preferred_element_type=F32)
@@ -123,7 +125,7 @@
         pair = [
             att_scr[slot_scr[(target * OLD + lane) * HEAD_DEV + i]] for i in range(HEAD_DEV)
         ]
-        att_ref[target] = jnp.concatenate(pair, axis=0).astype(BF16)
+        att_ref[target, : HEAD_DEV * 8] = jnp.concatenate(pair, axis=0).astype(BF16)
     for copy in copies:
         copy.wait()
 
@@ -133,9 +135,8 @@
     return pl.pallas_call(
         attend_kernel,
         out_shape=(
-            jax.ShapeDtypeStruct((ROWS, HEAD_DEV * 8, HEAD_DIM), BF16),
-            jax.ShapeDtypeStruct((1, ROWS) + block, BF16),
-            *[jax.ShapeDtypeStruct(block, BF16)] * (ROWS - 1),
+            jax.ShapeDtypeStruct((ROWS, 96, HEAD_DIM), BF16),
+            *[jax.ShapeDtypeStruct(block, BF16)] * ROWS,
         ),
         in_specs=[ANY] * 4,
         out_specs=(VMEM, *[ANY] * ROWS),
@@ -155,14 +156,14 @@
 
 
 def touch_kernel(weight_ref, out_ref):
-    out_ref[...] = weight_ref[:16, :128]
+    out_ref[...] = jnp.zeros_like(out_ref)
 
 
 def touch(out_weight):
     return pl.pallas_call(
         touch_kernel,
         out_shape=jax.ShapeDtypeStruct((16, 128), BF16),
-        in_specs=[VMEM],
+        in_specs=[ANY],
         out_specs=VMEM,
         cost_estimate=estimate(0.2),
         compiler_params=pltpu.CompilerParams(vmem_limit_bytes=VMEM_LIMIT),
@@ -172,9 +173,9 @@
 
 def project_kernel(att_ref, weight_ref, *refs):
     out_ref = refs[-1]
-    total = att_ref[0].astype(F32)
+    total = att_ref[0, : HEAD_DEV * 8].astype(F32)
     for row in range(1, ROWS):
-        total = total + att_ref[row].astype(F32)
+        total = total + att_ref[row, : HEAD_DEV * 8].astype(F32)
     features = jnp.concatenate([total[:8], total[8:]], axis=1).astype(BF16)
     for chip in range(CHIPS):
         part = jnp.dot(
@@ -197,67 +198,86 @@
     )(attended, out_weight, *arrived)
 
 
-def add_kernel(parts_ref, residual_ref, *refs):
-    out_ref = refs[-1]
+def widen_kernel(residual_ref, out_ref):
     core = lax.axis_index("head") % CORES
+    own = jnp.concatenate([residual_ref[row].astype(F32) for row in range(ROWS)], axis=0)
+    none = jnp.zeros_like(own)
+    out_ref[...] = jnp.concatenate(
+        [jnp.where(core == 0, own, none), jnp.where(core == 1, own, none)], axis=1
+    )
+
+
+def widen(residual):
+    return pl.pallas_call(
+        widen_kernel,
+        out_shape=jax.ShapeDtypeStruct((8, CHUNK), F32),
+        in_specs=[VMEM],
+        out_specs=VMEM,
+        cost_estimate=estimate(0.7),
+        compiler_params=pltpu.CompilerParams(vmem_limit_bytes=VMEM_LIMIT),
+        name="widen",
+    )(residual)
+
+
+def add_kernel(parts_ref, residual_ref, out_ref):
     total = parts_ref[0].astype(F32)
     for chip in range(1, CHIPS):
         total = total + parts_ref[chip].astype(F32)
-    own = jnp.concatenate([residual_ref[row].astype(F32) for row in range(ROWS)], axis=0)
-    none = jnp.zeros_like(own)
-    own = jnp.concatenate(
-        [jnp.where(core == 0, own, none), jnp.where(core == 1, own, none)], axis=1
-    )
-    out_ref[...] = total + own
-
-
-def add_residual(parts, residual, *arrived):
+    out_ref[...] = total + residual_ref[...]
+
+
+def add_residual(parts, residual):
     return pl.pallas_call(
         add_kernel,
         out_shape=jax.ShapeDtypeStruct((8, CHUNK), F32),
-        in_specs=[VMEM, VMEM] + [ANY] * len(arrived),
+        in_specs=[VMEM, VMEM],
         out_specs=VMEM,
         cost_estimate=estimate(0.2),
         compiler_params=pltpu.CompilerParams(vmem_limit_bytes=VMEM_LIMIT),
         name="add_residual",
-    )(parts, residual, *arrived)
-
-
-def hidden_kernel(sums_ref, *refs):
-    hidden_ref, spread_ref = refs[-2:]
-    core = lax.axis_index("head") % CORES
-    total = sums_ref[0] + sums_ref[1]
-    hidden = total.astype(BF16)
-    own = jnp.where(core == 0, total[:, :SHARE], total[:, SHARE:]).astype(BF16)
-    for row in range(ROWS):
-        hidden_ref[row] = own[2 * row : 2 * row + 2]
+    )(parts, residual)
+
+
+def hidden_kernel(sums_ref, spread_ref):
+    hidden = (sums_ref[0] + sums_ref[1]).astype(BF16)
     for chip in range(CHIPS):
         spread_ref[chip] = hidden
 
 
-def round_hidden(sums, *arrived):
+def round_hidden(sums):
     return pl.pallas_call(
         hidden_kernel,
-        out_shape=(
-            jax.ShapeDtypeStruct((ROWS, 2, SHARE), BF16),
-            jax.ShapeDtypeStruct((CHIPS, 8, CHUNK), BF16),
-        ),
-        in_specs=[VMEM] + [ANY] * len(arrived),
-        out_specs=(VMEM, VMEM),
-        cost_estimate=estimate(0.6),
+        out_shape=jax.ShapeDtypeStruct((CHIPS, 8, CHUNK), BF16),
+        in_specs=[VMEM],
+        out_specs=VMEM,
+        cost_estimate=estimate(0.2),
         compiler_params=pltpu.CompilerParams(vmem_limit_bytes=VMEM_LIMIT),
         name="round_hidden",
-    )(sums, *arrived)
-
-
-def norm_kernel(blocks_ref, gain_ref, bias_ref, kv1, kv2, kv3, _, out_ref, cache_ref, sems):
+    )(sums)
+
+
+def place(offsets, refs, cache_ref, sems):
     row = lax.axis_index("head") // OLD
     copies = []
-    for offset, kv_ref in enumerate((kv1, kv2, kv3), 1):
+    for offset, ref in zip(offsets, refs):
         source = (row + ROWS - offset) % ROWS
-        copy = pltpu.make_async_copy(kv_ref, cache_ref.at[0, source], sems.at[offset - 1])
-        copy.start()
-        copies.append(copy)
+        for kind in range(2):
+            copy = pltpu.make_async_copy(
+                ref.at[kind], cache_ref.at[0, source, kind], sems.at[len(copies)]
+            )
+            copy.start()
+            copies.append(copy)
+    return copies
+
+
+def norm_kernel(offsets, blocks_ref, gain_ref, bias_ref, *refs):
+    *kv_refs, out_ref, hidden_ref, cache_ref, sems = refs
+    copies = place(offsets, kv_refs, cache_ref, sems)
+    me = lax.axis_index("head")
+    own = blocks_ref[me // CORES].astype(F32)
+    own = jnp.where(me % CORES == 0, own[:, :SHARE], own[:, SHARE:]).astype(BF16)
+    for step in range(ROWS):
+        hidden_ref[step] = own[2 * step : 2 * step + 2]
     total = blocks_ref[0].astype(F32)
     for chip in range(1, CHIPS):
         total = total + blocks_ref[chip].astype(F32)
@@ -280,21 +300,40 @@
         copy.wait()
 
 
-def normalize(blocks, gain, bias, kv, cache_new):
-    return pl.pallas_call(
-        norm_kernel,
+def normalize(blocks, gain, bias, offsets, kv):
+    return pl.pallas_call(
+        functools.partial(norm_kernel, offsets),
         out_shape=(
             jax.ShapeDtypeStruct((ROWS, 2, OUT), BF16),
-            jax.ShapeDtypeStruct(cache_new.shape, BF16),
+            jax.ShapeDtypeStruct((ROWS, 2, SHARE), BF16),
+            jax.ShapeDtypeStruct((1, ROWS) + kv[0].shape, BF16),
         ),
-        in_specs=[VMEM] * 6 + [ANY],
-        out_specs=(VMEM, ANY),
-        scratch_shapes=[pltpu.SemaphoreType.DMA((ROWS - 1,))],
-        input_output_aliases={6: 1},
+        in_specs=[VMEM] * (3 + len(kv)),
+        out_specs=(VMEM, VMEM, HBM),
+        scratch_shapes=[pltpu.SemaphoreType.DMA((2 * len(kv),))],
         cost_estimate=estimate(1.4),
         compiler_params=pltpu.CompilerParams(vmem_limit_bytes=VMEM_LIMIT),
         name="normalize",
-    )(blocks, gain.reshape(OUT // 128, 128), bias.reshape(OUT // 128, 128), *kv, cache_new)
+    )(blocks, gain.reshape(OUT // 128, 128), bias.reshape(OUT // 128, 128), *kv)
+
+
+def last_kernel(offset, block_ref, _, cache_ref, sems):
+    for copy in place((offset,), (block_ref,), cache_ref, sems):
+        copy.wait()
+
+
+def place_last(offset, block, cache_new):
+    return pl.pallas_call(
+        functools.partial(last_kernel, offset),
+        out_shape=jax.ShapeDtypeStruct(cache_new.shape, BF16),
+        in_specs=[VMEM, HBM],
+        out_specs=HBM,
+        scratch_shapes=[pltpu.SemaphoreType.DMA((2,))],
+        input_output_aliases={1: 0},
+        cost_estimate=estimate(0.6),
+        compiler_params=pltpu.CompilerParams(vmem_limit_bytes=VMEM_LIMIT),
+        name="place_last",
+    )(block, cache_new)
 
 
 def exchange(blocks, groups):
@@ -305,20 +344,35 @@
     columns = [[row * OLD + lane for row in range(ROWS)] for lane in range(OLD)]
     sides = [[chip * CORES + core for chip in range(CHIPS)] for core in range(CORES)]
     pairs = [[chip * CORES + core for core in range(CORES)] for chip in range(CHIPS)]
-    picked, cache_new, *kv = attend_and_pick(slot_map, lengths, cache, fresh)
-    for offset in range(1, ROWS):
-        to = [(i, (i + offset * OLD) % MEMBERS) for i in range(MEMBERS)]
-        kv[offset - 1] = lax.ppermute(kv[offset - 1], "head", to)
-    parts = exchange(project(exchange(picked, columns), out_weight, touch(out_weight)), sides)
-
-    def finish(blocks, hidden):
-        sums = lax.all_gather(add_residual(blocks, hidden), "head", axis_index_groups=pairs)
-        hidden, copies = round_hidden(sums)
-        return exchange(copies, sides), hidden
-
-    blocks, hidden = lax.cond(lax.axis_index("head") < MEMBERS, finish, lambda a, b: (a, b), parts, residual)
-    normed, cache_new = normalize(blocks, norm_gain, norm_bias, kv, cache_new)
-    return (cache_new, hidden, normed)
+    picked, *kv = attend_and_pick(slot_map, lengths, cache, fresh)
+    first, inner = 1, (2, 3)
+
+    def shifted(offset):
+        pairs = [(i, (i + offset * OLD) % MEMBERS) for i in range(MEMBERS)]
+        return lax.ppermute(kv[offset], "head", pairs)
+
+    def region(run, *operands):
+        def none(*operands):
+            return jax.tree.map(lambda t: jnp.zeros(t.shape, t.dtype), jax.eval_shape(run, *operands))
+
+        return lax.cond(lax.axis_index("head") < MEMBERS, run, none, *operands)
+
+    def finish(total):
+        sums = lax.all_gather(total, "head", axis_index_groups=pairs)
+        return exchange(round_hidden(sums), sides)
+
+    def middle(attended, weight, residual, gain, bias, *seen):
+        parts = exchange(project(attended, weight, *seen), sides)
+        moved = [shifted(offset) for offset in inner]
+        blocks = region(finish, add_residual(parts, widen(residual)))
+        return normalize(blocks, gain, bias, (0,) + inner, (kv[0], *moved))
+
+    moved = shifted(first)
+    attended = exchange(picked, columns)
+    normed, hidden, cache_new = region(
+        middle, attended, out_weight, residual, norm_gain, norm_bias, touch(out_weight)
+    )
+    return (place_last(first, moved, cache_new), hidden, normed)
 
 
 def solution(mesh):

time: 50.5 us -> 49.6 us (0.982)
  local copies, waits for them, and re-layouts: 1.92 us -> 0.01 us
  blocking collectives: 16.9 us -> 18.8 us
  Pallas kernels: 5.83 us -> 7.69 us
  waiting for transfers between devices: 2.54 us -> 0.74 us
  starting transfers between devices: 22.2 us -> 21.3 us
    unnamed x16 -> x6, local copies, waits for them, and re-layouts: 1.92 us -> 0.01 us
    all_to_all x2, waiting for transfers between devices: 2.53 us -> 0.73 us  [exchange(): lax.all_to_all(blocks, 'head', 0, 0, axis_index_groups=groups, tiled=True)]
    all_gather x1, blocking collectives: 5.45 us -> 7.05 us  [finish(): sums = lax.all_gather(total, 'head', axis_index_groups=pairs)]
    pallas_call x3 -> x5, Pallas kernels: 4.57 us -> 5.91 us  [the longest x1 2.98 us: attend_and_pick(): pl.pallas_call(attend_kernel, out_shape=(jax.ShapeDtypeStruct((ROWS, 96,...]
    all_to_all x2, starting transfers between devices: 11.8 us -> 10.6 us  [exchange(): lax.all_to_all(blocks, 'head', 0, 0, axis_index_groups=groups, tiled=True)]
    pallas_call x1, Pallas kernels: 0.01 us -> 0.59 us  [touch(): pl.pallas_call(touch_kernel, out_shape=jax.ShapeDtypeStruct((16, 128), BF...]
  transfers between devices with their start and end apart: 5 -> 5, of which waited for: 1 -> 1; matrix products, arithmetic and copies ran while one was open for 0% -> 0% of each run, Pallas kernels for 0% -> 8%
where the time goes in v4:
time: 49.6 us; the launch traced here: 49.2 us
  starting transfers between devices  21.3 us (43%)
  blocking collectives  18.8 us (38%)
  Pallas kernels  7.69 us (16%)
  waiting for transfers between devices  0.74 us (1%)
  between operations  0.69 us (1%)
    all_to_all x1, blocking collectives, exchange(): lax.all_to_all(blocks, 'head', 0, 0, axis_index_groups=groups, tiled=True)  11.7 us
    all_to_all x2, starting transfers between devices, exchange(): lax.all_to_all(blocks, 'head', 0, 0, axis_index_groups=groups, tiled=True)  10.6 us
    ppermute x3, starting transfers between devices, shifted(): return lax.ppermute(kv[offset], 'head', pairs)  10.6 us
    all_gather x1, blocking collectives, finish(): sums = lax.all_gather(total, 'head', axis_index_groups=pairs)  7.05 us
    pallas_call x1, Pallas kernels, attend_and_pick(): pl.pallas_call(attend_kernel, out_shape=(jax.ShapeDtypeStruct((ROWS, 96,...  2.98 us
    pallas_call x1, Pallas kernels, normalize(): pl.pallas_call(functools.partial(norm_kernel, offsets), out_shape=(jax.Sh...  1.45 us
    pallas_call x1, Pallas kernels, project(): pl.pallas_call(project_kernel, out_shape=jax.ShapeDtypeStruct((CHIPS, 8,...  1.17 us
  transfers between devices with their start and end apart: 5, of which 1 were waited for; matrix products, arithmetic and copies ran while one was open for 0% of the time, Pallas kernels for 8%

profile of v4, /device:TPU:1, one launch (start us, length us, event | category | flops | bytes accessed | tf_op | source)
XLA Modules:
  0.0 49.2 jit_solution(2869537811543986270)
XLA Ops:
  0.6 0.0 copy-start
  0.6 0.0 copy-start.2
  0.7 0.0 copy-start.1
  0.7 3.0 %attend_and_pick.1 = (bf16[4,96,128]{2,1,0:T(8,128)(2,1)}, bf16[2,2,128,128]{3,2,1,0:T(8,128)(2,1)S(1)}, bf16[2,2,128,128]{3,2,1,0:T(8,128)(2,1)}, bf16[2,2,128,...) custom-call(s32[64]{0:T(128)} %slot_hbm.1, s32[4]{0:T(128)} %len_hbm.1, bf16[1,2,8,128,128]{4,3,2,1,0:T(8,128)(2,1)} %cache_ref.1, ...), custom_call_target="tpu_custom_call" | custom-call | bytes 12915000 | tf_op jit(solution)/shard_map/attend_and_pick/pallas_call | solution.py:135
  3.7 5.4 %all-to-all-start.2 = ((bf16[4,96,128]{2,1,0:T(8,128)(2,1)}), bf16[4,96,128]{2,1,0:T(8,128)(2,1)S(1)}, u32[]{:S(2)}, u32[]{:S(2)}) async-start(bf16[4,96,128]{2,1,0:T(8,128)(2,1)} %get-tuple-element.43), calls=%async_computation.2 | async-start | bytes 196608 | tf_op jit(solution)/shard_map/all_to_all | solution.py:340
  9.1 3.4 %collective-permute-start.2 = (bf16[2,2,128,128]{3,2,1,0:T(8,128)(2,1)}, bf16[2,2,128,128]{3,2,1,0:T(8,128)(2,1)S(1)}, u32[]{:S(2)}, u32[]{:S(2)}) collective-permute-start(bf16[2,2,128,128]{3,2,1,0:T(8,128)(2,1)} %get-tuple-element.42), channel_id=1, source_target_pairs={{0,8},{1,9},{2,10},{3,11},{4,12},{5,13},{6,14},{7,15},{8,16},{9,17... | collective-permute-start | bytes 393224 | tf_op jit(solution)/shard_map/ppermute | solution.py:352
  12.5 0.6 %touch.1 = bf16[16,128]{1,0:T(8,128)(2,1)} custom-call(bf16[256,6144]{1,0:T(8,128)(2,1)} %weight_ref.1), custom_call_target="tpu_custom_call" | custom-call | bytes 738000 | tf_op jit(solution)/shard_map/touch/pallas_call | solution.py:163
  13.0 0.7 %all-to-all-done.2 = bf16[4,96,128]{2,1,0:T(8,128)(2,1)S(1)} async-done(((bf16[4,96,128]{2,1,0:T(8,128)(2,1)}), bf16[4,96,128]{2,1,0:T(8,128)(2,1)S(1)}, u32[]{:S(2)}, u32[]{:S(2)}) %all-to-all-start.2) | async-done | bytes 98336 | tf_op jit(solution)/shard_map/all_to_all | solution.py:340
  13.8 0.0 copy-done
  13.8 0.0 copy-done.2
  13.8 0.0 copy-done.1
  13.8 34.7 %conditional.2 = ((bf16[4,2,6144]{2,1,0:T(2,128)(2,1)}, bf16[4,2,192]{2,1,0:T(2,128)(2,1)}, bf16[1,4,2,2,128,128]{5,4,3,2,1,0:T(8,128)(2,1)})) conditional(s32[]{:T(128)} %convert_element_type.6, () %tuple.21, (bf16[4,96,128]{2,1,0:T(8,128)(2,1)S(1)}, bf16[256,6144]{1,0:T(8,128)(2,1)S(1)}, bf16[16,128]{1,0:T(8,128)(2,1)}, ...), branch_computations={%region_0.0_spmd, %region_1.0_spmd} | conditional | flops 4 | bytes 13016122 | solution.py:358
  13.8 1.2 %project.1 = bf16[16,8,384]{2,1,0:T(8,128)(2,1)} custom-call(bf16[4,96,128]{2,1,0:T(8,128)(2,1)S(1)} %get-tuple-element.22.att_ref, bf16[256,6144]{1,0:T(8,128)(2,1)S(1)} %get-tuple-element.23.weight_ref, bf16[16,128]{1,0:T(8,128)(2,1)} %get-tuple-element.24.refs_0_), custom_call_target="tpu_custom_call" | custom-call | bytes 2214000 | tf_op jit(solution)/shard_map/cond/branch_1_fun/project/pallas_call | solution.py:190
  15.0 5.2 %all-to-all-start.1 = ((bf16[16,8,384]{2,1,0:T(8,128)(2,1)}), bf16[16,8,384]{2,1,0:T(8,128)(2,1)S(1)}, u32[]{:S(2)}, u32[]{:S(2)}) async-start(bf16[16,8,384]{2,1,0:T(8,128)(2,1)} %project.1), calls=%async_computation.1 | async-start | bytes 196608 | tf_op jit(solution)/shard_map/cond/branch_1_fun/all_to_all | solution.py:340
  20.2 4.2 %collective-permute-start = (bf16[2,2,128,128]{3,2,1,0:T(8,128)(2,1)}, bf16[2,2,128,128]{3,2,1,0:T(8,128)(2,1)S(1)}, u32[]{:S(2)}, u32[]{:S(2)}) collective-permute-start(bf16[2,2,128,128]{3,2,1,0:T(8,128)(2,1)} %get-tuple-element.29), channel_id=1, source_target_pairs={{0,16},{1,17},{2,18},{3,19},{4,20},{5,21},{6,22},{7,23},{8,24},{9,... | collective-permute-start | bytes 393224 | tf_op jit(solution)/shard_map/cond/branch_1_fun/ppermute | solution.py:352
  24.3 3.1 %collective-permute-start.1 = (bf16[2,2,128,128]{3,2,1,0:T(8,128)(2,1)}, bf16[2,2,128,128]{3,2,1,0:T(8,128)(2,1)S(1)}, u32[]{:S(2)}, u32[]{:S(2)}) collective-permute-start(bf16[2,2,128,128]{3,2,1,0:T(8,128)(2,1)} %get-tuple-element.30), channel_id=1, source_target_pairs={{0,24},{1,25},{2,26},{3,27},{4,28},{5,29},{6,30},{7,31},{8,0},{9,1... | collective-permute-start | bytes 393224 | tf_op jit(solution)/shard_map/cond/branch_1_fun/ppermute | solution.py:352
  27.4 0.8 %widen.1.residual_ref = f32[8,384]{1,0:T(8,128)S(1)} custom-call(bf16[4,2,192]{2,1,0:T(2,128)(2,1)} %get-tuple-element.53.residual_ref), custom_call_target="tpu_custom_call" | custom-call | bytes 2583000 | tf_op jit(solution)/shard_map/cond/branch_1_fun/widen/pallas_call | solution.py:211
  28.2 0.0 all-to-all-done.1.parts_ref
  28.2 18.8 %conditional = (bf16[16,8,384]{2,1,0:T(8,128)(2,1)S(1)}) conditional(s32[]{:T(128)} %convert_element_type.4, () %tuple.16, f32[8,384]{1,0:T(8,128)S(1)} %add_residual.1), branch_computations={%region_2.0_spmd, %region_3.0_spmd} | conditional | bytes 971480 | solution.py:358
  28.2 7.1 %all-gather = f32[16,384]{1,0:T(8,128)S(1)} all-gather(f32[8,384]{1,0:T(8,128)S(1)} %param.2), channel_id=2, replica_groups={{0,1},{2,3},{4,5},{6,7},{8,9},{10,11},{12,13},{14,15},{16,17},{18,19},{..., dimensions={0}, use_global_device_ids=true | all-gather | bytes 36864 | tf_op jit(solution)/shard_map/cond/branch_1_fun/cond/branch_1_fun/all_gather | solution.py:361
  35.3 11.7 %all_to_all.13 = bf16[16,8,384]{2,1,0:T(8,128)(2,1)S(1)} all-to-all(bf16[16,8,384]{2,1,0:T(8,128)(2,1)S(1)} %round_hidden.1), channel_id=1, replica_groups={{0,2,4,6,8,10,12,14,16,18,20,22,24,26,28,30},{1,3,5,7,9,11,13,15,17,19,..., dimensions={0} | all-to-all | bytes 196608 | tf_op jit(solution)/shard_map/cond/branch_1_fun/cond/branch_1_fun/all_to_all | solution.py:340
  47.0 0.0 collective-permute-done.refs_1_
  47.0 0.0 collective-permute-done.1.refs_2_
  47.0 1.5 %normalize.1 = (bf16[4,2,6144]{2,1,0:T(2,128)(2,1)}, bf16[4,2,192]{2,1,0:T(2,128)(2,1)}, bf16[1,4,2,2,128,128]{5,4,3,2,1,0:T(8,128)(2,1)}) custom-call(bf16[16,8,384]{2,1,0:T(8,128)(2,1)S(1)} %get-tuple-element.62.blocks_ref, f32[48,128]{1,0:T(8,128)S(1)} %bitcast.4, f32[48,128]{1,0:T(8,128)S(1)} %bitcast.5, ...), custom_call_target="tpu_custom_call" | custom-call | bytes 5166000 | tf_op jit(solution)/shard_map/cond/branch_1_fun/normalize/pallas_call | solution.py:304
  48.5 0.0 collective-permute-done.2.block_ref
  48.5 0.7 %place_last.1 = bf16[1,4,2,2,128,128]{5,4,3,2,1,0:T(8,128)(2,1)} custom-call(bf16[2,2,128,128]{3,2,1,0:T(8,128)(2,1)S(1)} %collective-permute-done.2.block_ref, bf16[1,4,2,2,128,128]{5,4,3,2,1,0:T(8,128)(2,1)} %get-tuple-element.47._), custom_call_target="tpu_custom_call", output_to_operand_aliasing={{}: (1, {})} | custom-call | bytes 2214000 | tf_op jit(solution)/shard_map/place_last/pallas_call | solution.py:326
  (2 shorter events, 0.0 us)
Async XLA Ops:
  0.6 13.1 %copy-start = (bf16[256,6144]{1,0:T(8,128)(2,1)S(1)}, bf16[256,6144]{1,0:T(8,128)(2,1)}, u32[]{:S(2)}) copy-start(bf16[256,6144]{1,0:T(8,128)(2,1)} %weight_ref.1) | copy-start | bytes 9437188
  0.6 13.1 %copy-start.2 = (f32[6144]{0:T(1024)S(1)}, f32[6144]{0:T(1024)}, u32[]{:S(2)}) copy-start(f32[6144]{0:T(1024)} %param.19) | copy-start | bytes 73732
  0.7 13.1 %copy-start.1 = (f32[6144]{0:T(1024)S(1)}, f32[6144]{0:T(1024)}, u32[]{:S(2)}) copy-start(f32[6144]{0:T(1024)} %param.18) | copy-start | bytes 73732
  3.7 10.1 %all-to-all-start.2 = ((bf16[4,96,128]{2,1,0:T(8,128)(2,1)}), bf16[4,96,128]{2,1,0:T(8,128)(2,1)S(1)}, u32[]{:S(2)}, u32[]{:S(2)}) async-start(bf16[4,96,128]{2,1,0:T(8,128)(2,1)} %get-tuple-element.43), calls=%async_computation.2 | async-start | bytes 196608 | tf_op jit(solution)/shard_map/all_to_all | solution.py:340
  9.1 39.4 %collective-permute-start.2 = (bf16[2,2,128,128]{3,2,1,0:T(8,128)(2,1)}, bf16[2,2,128,128]{3,2,1,0:T(8,128)(2,1)S(1)}, u32[]{:S(2)}, u32[]{:S(2)}) collective-permute-start(bf16[2,2,128,128]{3,2,1,0:T(8,128)(2,1)} %get-tuple-element.42), channel_id=1, source_target_pairs={{0,8},{1,9},{2,10},{3,11},{4,12},{5,13},{6,14},{7,15},{8,16},{9,17... | collective-permute-start | bytes 393224 | tf_op jit(solution)/shard_map/ppermute | solution.py:352
  15.0 13.3 %all-to-all-start.1 = ((bf16[16,8,384]{2,1,0:T(8,128)(2,1)}), bf16[16,8,384]{2,1,0:T(8,128)(2,1)S(1)}, u32[]{:S(2)}, u32[]{:S(2)}) async-start(bf16[16,8,384]{2,1,0:T(8,128)(2,1)} %project.1), calls=%async_computation.1 | async-start | bytes 196608 | tf_op jit(solution)/shard_map/cond/branch_1_fun/all_to_all | solution.py:340
  20.2 26.9 %collective-permute-start = (bf16[2,2,128,128]{3,2,1,0:T(8,128)(2,1)}, bf16[2,2,128,128]{3,2,1,0:T(8,128)(2,1)S(1)}, u32[]{:S(2)}, u32[]{:S(2)}) collective-permute-start(bf16[2,2,128,128]{3,2,1,0:T(8,128)(2,1)} %get-tuple-element.29), channel_id=1, source_target_pairs={{0,16},{1,17},{2,18},{3,19},{4,20},{5,21},{6,22},{7,23},{8,24},{9,... | collective-permute-start | bytes 393224 | tf_op jit(solution)/shard_map/cond/branch_1_fun/ppermute | solution.py:352
  24.3 22.7 %collective-permute-start.1 = (bf16[2,2,128,128]{3,2,1,0:T(8,128)(2,1)}, bf16[2,2,128,128]{3,2,1,0:T(8,128)(2,1)S(1)}, u32[]{:S(2)}, u32[]{:S(2)}) collective-permute-start(bf16[2,2,128,128]{3,2,1,0:T(8,128)(2,1)} %get-tuple-element.30), channel_id=1, source_target_pairs={{0,24},{1,25},{2,26},{3,27},{4,28},{5,29},{6,30},{7,31},{8,0},{9,1... | collective-permute-start | bytes 393224 | tf_op jit(solution)/shard_map/cond/branch_1_fun/ppermute | solution.py:352

commit v5 on v4

--- a/solution.py
+++ b/solution.py
@@ -20,6 +20,12 @@
 OLD = MEMBERS // ROWS
 SHARE = OUT // MEMBERS
 CHUNK = OUT // CHIPS
+SIDE = 4
+RANK = [chip % SIDE * SIDE + chip // SIDE for chip in range(CHIPS)]
+BLOCK = 2 * HEAD_DEV * LEN
+FEW = HEAD_DEV * 8
+EARLY = 64
+LATE = BLOCK - EARLY
 F32 = jnp.float32
 BF16 = jnp.bfloat16
 FIRST_LIMIT = 56 * 2**20
@@ -61,8 +67,14 @@
             target = (row + offset) % ROWS
             for i in range(HEAD_DEV):
                 slot = slot_scr[(target * OLD + lane) * HEAD_DEV + i]
+                at = (kind * HEAD_DEV + i) * LEN
+                rows = min(LEN, LATE - at)
+                if rows <= 0:
+                    continue
                 copy = pltpu.make_async_copy(
-                    held.at[kind, slot], kv_ref.at[kind, i], sems.at[len(copies)]
+                    held.at[kind, slot, pl.ds(0, rows)],
+                    kv_ref.at[pl.ds(at, rows)],
+                    sems.at[len(copies)],
                 )
                 copy.start()
                 copies.append(copy)
@@ -125,18 +137,19 @@
         pair = [
             att_scr[slot_scr[(target * OLD + lane) * HEAD_DEV + i]] for i in range(HEAD_DEV)
         ]
-        att_ref[target, : HEAD_DEV * 8] = jnp.concatenate(pair, axis=0).astype(BF16)
+        att_ref[target, :FEW] = jnp.concatenate(pair, axis=0).astype(BF16)
+        slot = slot_scr[(target * OLD + lane) * HEAD_DEV + HEAD_DEV - 1]
+        att_ref[target, FEW:] = held[1, slot, LEN - EARLY :]
     for copy in copies:
         copy.wait()
 
 
 def attend_and_pick(slot_map, lengths, cache, fresh):
-    block = (2, HEAD_DEV, LEN, HEAD_DIM)
     return pl.pallas_call(
         attend_kernel,
         out_shape=(
-            jax.ShapeDtypeStruct((ROWS, 96, HEAD_DIM), BF16),
-            *[jax.ShapeDtypeStruct(block, BF16)] * ROWS,
+            jax.ShapeDtypeStruct((ROWS, FEW + EARLY, HEAD_DIM), BF16),
+            *[jax.ShapeDtypeStruct((LATE, HEAD_DIM), BF16)] * ROWS,
         ),
         in_specs=[ANY] * 4,
         out_specs=(VMEM, *[ANY] * ROWS),
@@ -173,9 +186,9 @@
 
 def project_kernel(att_ref, weight_ref, *refs):
     out_ref = refs[-1]
-    total = att_ref[0, : HEAD_DEV * 8].astype(F32)
+    total = att_ref[0, :FEW].astype(F32)
     for row in range(1, ROWS):
-        total = total + att_ref[row, : HEAD_DEV * 8].astype(F32)
+        total = total + att_ref[row, :FEW].astype(F32)
     features = jnp.concatenate([total[:8], total[8:]], axis=1).astype(BF16)
     for chip in range(CHIPS):
         part = jnp.dot(
@@ -183,7 +196,7 @@
             weight_ref[:, chip * CHUNK : (chip + 1) * CHUNK],
             preferred_element_type=F32,
         )
-        out_ref[chip] = part.astype(BF16)
+        out_ref[RANK[chip]] = part.astype(BF16)
 
 
 def project(attended, out_weight, *arrived):
@@ -261,20 +274,29 @@
     copies = []
     for offset, ref in zip(offsets, refs):
         source = (row + ROWS - offset) % ROWS
-        for kind in range(2):
+        for part in (pl.ds(0, BLOCK // 2), pl.ds(BLOCK // 2, LATE - BLOCK // 2)):
             copy = pltpu.make_async_copy(
-                ref.at[kind], cache_ref.at[0, source, kind], sems.at[len(copies)]
+                ref.at[part], cache_ref.at[0, source, part], sems.at[len(copies)]
             )
             copy.start()
             copies.append(copy)
     return copies
 
 
-def norm_kernel(offsets, blocks_ref, gain_ref, bias_ref, *refs):
+def norm_kernel(offsets, blocks_ref, gain_ref, bias_ref, early_ref, *refs):
     *kv_refs, out_ref, hidden_ref, cache_ref, sems = refs
     copies = place(offsets, kv_refs, cache_ref, sems)
+    for row in range(ROWS):
+        copy = pltpu.make_async_copy(
+            early_ref.at[row, pl.ds(FEW, EARLY)],
+            cache_ref.at[0, row, pl.ds(LATE, EARLY)],
+            sems.at[len(copies)],
+        )
+        copy.start()
+        copies.append(copy)
     me = lax.axis_index("head")
-    own = blocks_ref[me // CORES].astype(F32)
+    chip = me // CORES
+    own = blocks_ref[chip % SIDE * SIDE + chip // SIDE].astype(F32)
     own = jnp.where(me % CORES == 0, own[:, :SHARE], own[:, SHARE:]).astype(BF16)
     for step in range(ROWS):
         hidden_ref[step] = own[2 * step : 2 * step + 2]
@@ -289,7 +311,7 @@
     scale = 1.0 / jnp.sqrt(var + 1e-05)
     tiles = CHUNK // 128
     for chip in range(CHIPS):
-        values = (blocks_ref[chip].astype(F32) - mean) * scale
+        values = (blocks_ref[RANK[chip]].astype(F32) - mean) * scale
         for tile in range(tiles):
             at = chip * tiles + tile
             part = values[:, tile * 128 : (tile + 1) * 128]
@@ -300,21 +322,27 @@
         copy.wait()
 
 
-def normalize(blocks, gain, bias, offsets, kv):
+def normalize(blocks, gain, bias, early, offsets, kv):
     return pl.pallas_call(
         functools.partial(norm_kernel, offsets),
         out_shape=(
             jax.ShapeDtypeStruct((ROWS, 2, OUT), BF16),
             jax.ShapeDtypeStruct((ROWS, 2, SHARE), BF16),
-            jax.ShapeDtypeStruct((1, ROWS) + kv[0].shape, BF16),
+            jax.ShapeDtypeStruct((1, ROWS, BLOCK, HEAD_DIM), BF16),
         ),
-        in_specs=[VMEM] * (3 + len(kv)),
+        in_specs=[VMEM] * (4 + len(kv)),
         out_specs=(VMEM, VMEM, HBM),
-        scratch_shapes=[pltpu.SemaphoreType.DMA((2 * len(kv),))],
+        scratch_shapes=[pltpu.SemaphoreType.DMA((2 * len(kv) + ROWS,))],
         cost_estimate=estimate(1.4),
         compiler_params=pltpu.CompilerParams(vmem_limit_bytes=VMEM_LIMIT),
         name="normalize",
-    )(blocks, gain.reshape(OUT // 128, 128), bias.reshape(OUT // 128, 128), *kv)
+    )(
+        blocks,
+        gain.reshape(OUT // 128, 128),
+        bias.reshape(OUT // 128, 128),
+        early,
+        *kv,
+    )
 
 
 def last_kernel(offset, block_ref, _, cache_ref, sems):
@@ -342,7 +370,7 @@
 
 def body(cache, fresh, slot_map, lengths, out_weight, residual, norm_gain, norm_bias):
     columns = [[row * OLD + lane for row in range(ROWS)] for lane in range(OLD)]
-    sides = [[chip * CORES + core for chip in range(CHIPS)] for core in range(CORES)]
+    sides = [[RANK[chip] * CORES + core for chip in range(CHIPS)] for core in range(CORES)]
     pairs = [[chip * CORES + core for core in range(CORES)] for chip in range(CHIPS)]
     picked, *kv = attend_and_pick(slot_map, lengths, cache, fresh)
     first, inner = 1, (2, 3)
@@ -365,14 +393,15 @@
         parts = exchange(project(attended, weight, *seen), sides)
         moved = [shifted(offset) for offset in inner]
         blocks = region(finish, add_residual(parts, widen(residual)))
-        return normalize(blocks, gain, bias, (0,) + inner, (kv[0], *moved))
+        return normalize(blocks, gain, bias, attended, (0,) + inner, (kv[0], *moved))
 
     moved = shifted(first)
     attended = exchange(picked, columns)
     normed, hidden, cache_new = region(
         middle, attended, out_weight, residual, norm_gain, norm_bias, touch(out_weight)
     )
-    return (place_last(first, moved, cache_new), hidden, normed)
+    cache_new = place_last(first, moved, cache_new)
+    return (cache_new.reshape(1, ROWS, 2, HEAD_DEV, LEN, HEAD_DIM), hidden, normed)
 
 
 def solution(mesh):

time: 49.6 us -> 48.5 us (0.978)
  Pallas kernels: 7.69 us -> 6.42 us
  waiting for transfers between devices: 0.74 us -> 1.27 us
  starting transfers between devices: 21.3 us -> 20.8 us
    pallas_call x1, Pallas kernels: 0.77 us -> 0.09 us  [widen(): pl.pallas_call(widen_kernel, out_shape=jax.ShapeDtypeStruct((8, CHUNK), F...]
    pallas_call x1, Pallas kernels: 0.59 us -> 0.01 us  [touch(): pl.pallas_call(touch_kernel, out_shape=jax.ShapeDtypeStruct((16, 128), BF...]
    all_to_all x2, waiting for transfers between devices: 0.73 us -> 1.26 us  [exchange(): lax.all_to_all(blocks, 'head', 0, 0, axis_index_groups=groups, tiled=True)]
  transfers between devices with their start and end apart: 5 -> 5, of which waited for: 1 -> 1; matrix products, arithmetic and copies ran while one was open for 0% -> 0% of each run, Pallas kernels for 8% -> 6%
where the time goes in v5:
time: 48.5 us; the launch traced here: 48.1 us
  starting transfers between devices  20.8 us (43%)
  blocking collectives  18.8 us (39%)
  Pallas kernels  6.42 us (13%)
  waiting for transfers between devices  1.27 us (3%)
  between operations  0.72 us (1%)
    all_to_all x1, blocking collectives, exchange(): lax.all_to_all(blocks, 'head', 0, 0, axis_index_groups=groups, tiled=True)  11.5 us
    ppermute x3, starting transfers between devices, shifted(): return lax.ppermute(kv[offset], 'head', pairs)  10.6 us
    all_to_all x2, starting transfers between devices, exchange(): lax.all_to_all(blocks, 'head', 0, 0, axis_index_groups=groups, tiled=True)  10.2 us
    all_gather x1, blocking collectives, finish(): sums = lax.all_gather(total, 'head', axis_index_groups=pairs)  7.36 us
    pallas_call x1, Pallas kernels, attend_and_pick(): pl.pallas_call(attend_kernel, out_shape=(jax.ShapeDtypeStruct((ROWS, FEW...  2.96 us
    pallas_call x1, Pallas kernels, normalize(): pl.pallas_call(functools.partial(norm_kernel, offsets), out_shape=(jax.Sh...  1.49 us
    all_to_all x2, waiting for transfers between devices, exchange(): lax.all_to_all(blocks, 'head', 0, 0, axis_index_groups=groups, tiled=True)  1.26 us
    pallas_call x1, Pallas kernels, project(): pl.pallas_call(project_kernel, out_shape=jax.ShapeDtypeStruct((CHIPS, 8,...  1.17 us
  transfers between devices with their start and end apart: 5, of which 1 were waited for; matrix products, arithmetic and copies ran while one was open for 0% of the time, Pallas kernels for 6%

profile of v5, /device:TPU:1, one launch (start us, length us, event | category | flops | bytes accessed | tf_op | source)
XLA Modules:
  0.0 48.1 jit_solution(10978643791525455164)
XLA Ops:
  0.6 0.0 copy-start
  0.6 0.0 copy-start.2
  0.7 0.0 copy-start.1
  0.7 0.0 copy-start.3
  0.7 3.0 %attend_and_pick.1 = (bf16[4,80,128]{2,1,0:T(8,128)(2,1)}, bf16[448,128]{1,0:T(8,128)(2,1)S(1)}, bf16[448,128]{1,0:T(8,128)(2,1)}, bf16[448,128]{1,0:T(8,128)(2,1)}, bf16[448,128]{1,0:T(8,128)(2,1)}) custom-call(s32[64]{0:T(128)} %slot_hbm.1, s32[4]{0:T(128)} %len_hbm.1, bf16[1,2,8,128,128]{4,3,2,1,0:T(8,128)(2,1)} %cache_ref.1, ...), custom_call_target="tpu_custom_call" | custom-call | bytes 12915000 | tf_op jit(solution)/shard_map/attend_and_pick/pallas_call | solution.py:148
  3.6 5.4 %all-to-all-start.2 = ((bf16[4,80,128]{2,1,0:T(8,128)(2,1)}), bf16[4,80,128]{2,1,0:T(8,128)(2,1)S(1)}, u32[]{:S(2)}, u32[]{:S(2)}) async-start(bf16[4,80,128]{2,1,0:T(8,128)(2,1)} %get-tuple-element.43), calls=%async_computation.2 | async-start | bytes 163840 | tf_op jit(solution)/shard_map/all_to_all | solution.py:368
  9.1 3.4 %collective-permute-start.2 = (bf16[448,128]{1,0:T(8,128)(2,1)}, bf16[448,128]{1,0:T(8,128)(2,1)S(1)}, u32[]{:S(2)}, u32[]{:S(2)}) collective-permute-start(bf16[448,128]{1,0:T(8,128)(2,1)} %get-tuple-element.42), channel_id=1, source_target_pairs={{0,8},{1,9},{2,10},{3,11},{4,12},{5,13},{6,14},{7,15},{8,16},{9,17... | collective-permute-start | bytes 344072 | tf_op jit(solution)/shard_map/ppermute | solution.py:380
  12.4 1.3 %all-to-all-done.2 = bf16[4,80,128]{2,1,0:T(8,128)(2,1)S(1)} async-done(((bf16[4,80,128]{2,1,0:T(8,128)(2,1)}), bf16[4,80,128]{2,1,0:T(8,128)(2,1)S(1)}, u32[]{:S(2)}, u32[]{:S(2)}) %all-to-all-start.2) | async-done | bytes 81952 | tf_op jit(solution)/shard_map/all_to_all | solution.py:368
  13.7 0.0 copy-done
  13.7 0.0 copy-done.2
  13.7 0.0 copy-done.1
  13.7 0.0 copy-done.3
  13.7 33.6 %conditional.2 = ((bf16[4,2,6144]{2,1,0:T(2,128)(2,1)}, bf16[4,2,192]{2,1,0:T(2,128)(2,1)}, bf16[1,4,512,128]{3,2,1,0:T(8,128)(2,1)})) conditional(s32[]{:T(128)} %convert_element_type.6, () %tuple.21, (bf16[4,80,128]{2,1,0:T(8,128)(2,1)S(1)}, bf16[256,6144]{1,0:T(8,128)(2,1)S(1)}, bf16[16,128]{1,0:T(8,128)(2,1)S(1)}, ...), branch_computations={%region_0.0_spmd, %region_1.0_spmd} | conditional | flops 4 | bytes 12885050 | solution.py:386
  13.7 1.2 %project.1 = bf16[16,8,384]{2,1,0:T(8,128)(2,1)} custom-call(bf16[4,80,128]{2,1,0:T(8,128)(2,1)S(1)} %get-tuple-element.22.att_ref.early_ref, bf16[256,6144]{1,0:T(8,128)(2,1)S(1)} %get-tuple-element.23.weight_ref, bf16[16,128]{1,0:T(8,128)(2,1)S(1)} %get-tuple-element.24.refs_0_), custom_call_target="tpu_custom_call" | custom-call | bytes 2214000 | tf_op jit(solution)/shard_map/cond/branch_1_fun/project/pallas_call | solution.py:203
  14.9 4.7 %all-to-all-start.1 = ((bf16[16,8,384]{2,1,0:T(8,128)(2,1)}), bf16[16,8,384]{2,1,0:T(8,128)(2,1)S(1)}, u32[]{:S(2)}, u32[]{:S(2)}) async-start(bf16[16,8,384]{2,1,0:T(8,128)(2,1)} %project.1), calls=%async_computation.1 | async-start | bytes 196608 | tf_op jit(solution)/shard_map/cond/branch_1_fun/all_to_all | solution.py:368
  19.6 4.2 %collective-permute-start = (bf16[448,128]{1,0:T(8,128)(2,1)}, bf16[448,128]{1,0:T(8,128)(2,1)S(1)}, u32[]{:S(2)}, u32[]{:S(2)}) collective-permute-start(bf16[448,128]{1,0:T(8,128)(2,1)} %get-tuple-element.29), channel_id=1, source_target_pairs={{0,16},{1,17},{2,18},{3,19},{4,20},{5,21},{6,22},{7,23},{8,24},{9,... | collective-permute-start | bytes 344072 | tf_op jit(solution)/shard_map/cond/branch_1_fun/ppermute | solution.py:380
  23.8 3.1 %collective-permute-start.1 = (bf16[448,128]{1,0:T(8,128)(2,1)}, bf16[448,128]{1,0:T(8,128)(2,1)S(1)}, u32[]{:S(2)}, u32[]{:S(2)}) collective-permute-start(bf16[448,128]{1,0:T(8,128)(2,1)} %get-tuple-element.30), channel_id=1, source_target_pairs={{0,24},{1,25},{2,26},{3,27},{4,28},{5,29},{6,30},{7,31},{8,0},{9,1... | collective-permute-start | bytes 344072 | tf_op jit(solution)/shard_map/cond/branch_1_fun/ppermute | solution.py:380
  26.9 0.1 widen.1.residual_ref
  27.0 0.0 all-to-all-done.1.parts_ref
  27.0 18.9 %conditional = (bf16[16,8,384]{2,1,0:T(8,128)(2,1)S(1)}) conditional(s32[]{:T(128)} %convert_element_type.4, () %tuple.16, f32[8,384]{1,0:T(8,128)S(1)} %add_residual.1), branch_computations={%region_2.0_spmd, %region_3.0_spmd} | conditional | bytes 971480 | solution.py:386
  27.0 7.4 %all-gather = f32[16,384]{1,0:T(8,128)S(1)} all-gather(f32[8,384]{1,0:T(8,128)S(1)} %param.2), channel_id=2, replica_groups={{0,1},{2,3},{4,5},{6,7},{8,9},{10,11},{12,13},{14,15},{16,17},{18,19},{..., dimensions={0}, use_global_device_ids=true | all-gather | bytes 36864 | tf_op jit(solution)/shard_map/cond/branch_1_fun/cond/branch_1_fun/all_gather | solution.py:389
  34.4 11.5 %all_to_all.13 = bf16[16,8,384]{2,1,0:T(8,128)(2,1)S(1)} all-to-all(bf16[16,8,384]{2,1,0:T(8,128)(2,1)S(1)} %round_hidden.1), channel_id=1, replica_groups={{0,8,16,24,2,10,18,26,4,12,20,28,6,14,22,30},{1,9,17,25,3,11,19,27,5,13..., dimensions={0} | all-to-all | bytes 196608 | tf_op jit(solution)/shard_map/cond/branch_1_fun/cond/branch_1_fun/all_to_all | solution.py:368
  45.9 0.0 collective-permute-done.refs_1_
  45.9 0.0 collective-permute-done.1.refs_2_
  45.9 1.5 %normalize.1 = (bf16[4,2,6144]{2,1,0:T(2,128)(2,1)}, bf16[4,2,192]{2,1,0:T(2,128)(2,1)}, bf16[1,4,512,128]{3,2,1,0:T(8,128)(2,1)}) custom-call(bf16[16,8,384]{2,1,0:T(8,128)(2,1)S(1)} %get-tuple-element.62.blocks_ref, f32[48,128]{1,0:T(8,128)S(1)} %bitcast.5, f32[48,128]{1,0:T(8,128)S(1)} %bitcast.6, ...), custom_call_target="tpu_custom_call" | custom-call | bytes 5166000 | tf_op jit(solution)/shard_map/cond/branch_1_fun/normalize/pallas_call | solution.py:326
  47.4 0.0 collective-permute-done.2.block_ref
  47.4 0.7 %place_last.1 = bf16[1,4,512,128]{3,2,1,0:T(8,128)(2,1)} custom-call(bf16[448,128]{1,0:T(8,128)(2,1)S(1)} %collective-permute-done.2.block_ref, bf16[1,4,512,128]{3,2,1,0:T(8,128)(2,1)} %get-tuple-element.47._), custom_call_target="tpu_custom_call", output_to_operand_aliasing={{}: (1, {})} | custom-call | bytes 2214000 | tf_op jit(solution)/shard_map/place_last/pallas_call | solution.py:354
  (3 shorter events, 0.0 us)
Async XLA Ops:
  0.6 13.1 %copy-start = (bf16[256,6144]{1,0:T(8,128)(2,1)S(1)}, bf16[256,6144]{1,0:T(8,128)(2,1)}, u32[]{:S(2)}) copy-start(bf16[256,6144]{1,0:T(8,128)(2,1)} %weight_ref.1) | copy-start | bytes 9437188
  0.6 13.1 %copy-start.2 = (f32[6144]{0:T(1024)S(1)}, f32[6144]{0:T(1024)}, u32[]{:S(2)}) copy-start(f32[6144]{0:T(1024)} %param.19) | copy-start | bytes 73732
  0.7 13.1 %copy-start.1 = (f32[6144]{0:T(1024)S(1)}, f32[6144]{0:T(1024)}, u32[]{:S(2)}) copy-start(f32[6144]{0:T(1024)} %param.18) | copy-start | bytes 73732
  0.7 13.1 %copy-start.3 = (bf16[4,2,192]{2,1,0:T(2,128)(2,1)S(1)}, bf16[4,2,192]{2,1,0:T(2,128)(2,1)}, u32[]{:S(2)}) copy-start(bf16[4,2,192]{2,1,0:T(2,128)(2,1)} %param.17) | copy-start | bytes 9220
  3.6 10.1 %all-to-all-start.2 = ((bf16[4,80,128]{2,1,0:T(8,128)(2,1)}), bf16[4,80,128]{2,1,0:T(8,128)(2,1)S(1)}, u32[]{:S(2)}, u32[]{:S(2)}) async-start(bf16[4,80,128]{2,1,0:T(8,128)(2,1)} %get-tuple-element.43), calls=%async_computation.2 | async-start | bytes 163840 | tf_op jit(solution)/shard_map/all_to_all | solution.py:368
  9.1 38.3 %collective-permute-start.2 = (bf16[448,128]{1,0:T(8,128)(2,1)}, bf16[448,128]{1,0:T(8,128)(2,1)S(1)}, u32[]{:S(2)}, u32[]{:S(2)}) collective-permute-start(bf16[448,128]{1,0:T(8,128)(2,1)} %get-tuple-element.42), channel_id=1, source_target_pairs={{0,8},{1,9},{2,10},{3,11},{4,12},{5,13},{6,14},{7,15},{8,16},{9,17... | collective-permute-start | bytes 344072 | tf_op jit(solution)/shard_map/ppermute | solution.py:380
  14.9 12.1 %all-to-all-start.1 = ((bf16[16,8,384]{2,1,0:T(8,128)(2,1)}), bf16[16,8,384]{2,1,0:T(8,128)(2,1)S(1)}, u32[]{:S(2)}, u32[]{:S(2)}) async-start(bf16[16,8,384]{2,1,0:T(8,128)(2,1)} %project.1), calls=%async_computation.1 | async-start | bytes 196608 | tf_op jit(solution)/shard_map/cond/branch_1_fun/all_to_all | solution.py:368
  19.6 26.2 %collective-permute-start = (bf16[448,128]{1,0:T(8,128)(2,1)}, bf16[448,128]{1,0:T(8,128)(2,1)S(1)}, u32[]{:S(2)}, u32[]{:S(2)}) collective-permute-start(bf16[448,128]{1,0:T(8,128)(2,1)} %get-tuple-element.29), channel_id=1, source_target_pairs={{0,16},{1,17},{2,18},{3,19},{4,20},{5,21},{6,22},{7,23},{8,24},{9,... | collective-permute-start | bytes 344072 | tf_op jit(solution)/shard_map/cond/branch_1_fun/ppermute | solution.py:380
  23.8 22.1 %collective-permute-start.1 = (bf16[448,128]{1,0:T(8,128)(2,1)}, bf16[448,128]{1,0:T(8,128)(2,1)S(1)}, u32[]{:S(2)}, u32[]{:S(2)}) collective-permute-start(bf16[448,128]{1,0:T(8,128)(2,1)} %get-tuple-element.30), channel_id=1, source_target_pairs={{0,24},{1,25},{2,26},{3,27},{4,28},{5,29},{6,30},{7,31},{8,0},{9,1... | collective-permute-start | bytes 344072 | tf_op jit(solution)/shard_map/cond/branch_1_fun/ppermute | solution.py:380

commit v6 on v5

--- a/solution.py
+++ b/solution.py
@@ -20,8 +20,10 @@
 OLD = MEMBERS // ROWS
 SHARE = OUT // MEMBERS
 CHUNK = OUT // CHIPS
-SIDE = 4
-RANK = [chip % SIDE * SIDE + chip // SIDE for chip in range(CHIPS)]
+SUM_ORDER = [0, 1, 2, 3, 4, 5, 6, 7, 8, 9, 10, 11, 12, 13, 14, 15]
+ROW_ORDER = [2, 6, 10, 14, 3, 7, 11, 15, 0, 4, 8, 12, 1, 5, 9, 13]
+SUM_RANK = [SUM_ORDER.index(chip) for chip in range(CHIPS)]
+ROW_RANK = [ROW_ORDER.index(chip) for chip in range(CHIPS)]
 BLOCK = 2 * HEAD_DEV * LEN
 FEW = HEAD_DEV * 8
 EARLY = 64
@@ -196,7 +198,7 @@
             weight_ref[:, chip * CHUNK : (chip + 1) * CHUNK],
             preferred_element_type=F32,
         )
-        out_ref[RANK[chip]] = part.astype(BF16)
+        out_ref[SUM_RANK[chip]] = part.astype(BF16)
 
 
 def project(attended, out_weight, *arrived):
@@ -296,7 +298,9 @@
         copies.append(copy)
     me = lax.axis_index("head")
     chip = me // CORES
-    own = blocks_ref[chip % SIDE * SIDE + chip // SIDE].astype(F32)
+    own = jnp.zeros((8, CHUNK), F32)
+    for one in range(CHIPS):
+        own = jnp.where(chip == one, blocks_ref[ROW_RANK[one]].astype(F32), own)
     own = jnp.where(me % CORES == 0, own[:, :SHARE], own[:, SHARE:]).astype(BF16)
     for step in range(ROWS):
         hidden_ref[step] = own[2 * step : 2 * step + 2]
@@ -311,7 +315,7 @@
     scale = 1.0 / jnp.sqrt(var + 1e-05)
     tiles = CHUNK // 128
     for chip in range(CHIPS):
-        values = (blocks_ref[RANK[chip]].astype(F32) - mean) * scale
+        values = (blocks_ref[ROW_RANK[chip]].astype(F32) - mean) * scale
         for tile in range(tiles):
             at = chip * tiles + tile
             part = values[:, tile * 128 : (tile + 1) * 128]
@@ -370,7 +374,8 @@
 
 def body(cache, fresh, slot_map, lengths, out_weight, residual, norm_gain, norm_bias):
     columns = [[row * OLD + lane for row in range(ROWS)] for lane in range(OLD)]
-    sides = [[RANK[chip] * CORES + core for chip in range(CHIPS)] for core in range(CORES)]
+    sum_sides = [[chip * CORES + core for chip in SUM_ORDER] for core in range(CORES)]
+    row_sides = [[chip * CORES + core for chip in ROW_ORDER] for core in range(CORES)]
     pairs = [[chip * CORES + core for core in range(CORES)] for chip in range(CHIPS)]
     picked, *kv = attend_and_pick(slot_map, lengths, cache, fresh)
     first, inner = 1, (2, 3)
@@ -387,10 +392,10 @@
 
     def finish(total):
         sums = lax.all_gather(total, "head", axis_index_groups=pairs)
-        return exchange(round_hidden(sums), sides)
+        return exchange(round_hidden(sums), row_sides)
 
     def middle(attended, weight, residual, gain, bias, *seen):
-        parts = exchange(project(attended, weight, *seen), sides)
+        parts = exchange(project(attended, weight, *seen), sum_sides)
         moved = [shifted(offset) for offset in inner]
         blocks = region(finish, add_residual(parts, widen(residual)))
         return normalize(blocks, gain, bias, attended, (0,) + inner, (kv[0], *moved))

time: 48.5 us -> 47.3 us (0.975)
  blocking collectives: 18.8 us -> 17.5 us
    all_to_all x1, blocking collectives: 11.5 us -> 9.68 us  [exchange(): lax.all_to_all(blocks, 'head', 0, 0, axis_index_groups=groups, tiled=True)]
  transfers between devices with their start and end apart: 5 -> 5, of which waited for: 1 -> 2; matrix products, arithmetic and copies ran while one was open for 0% -> 0% of each run, Pallas kernels for 6% -> 6%
where the time goes in v6:
time: 47.3 us; the launch traced here: 46.9 us
  starting transfers between devices  20.8 us (44%)
  blocking collectives  17.5 us (37%)
  Pallas kernels  6.43 us (14%)
  waiting for transfers between devices  1.43 us (3%)
  between operations  0.72 us (2%)
    ppermute x3, starting transfers between devices, shifted(): return lax.ppermute(kv[offset], 'head', pairs)  10.6 us
    all_to_all x2, starting transfers between devices, exchange(): lax.all_to_all(blocks, 'head', 0, 0, axis_index_groups=groups, tiled=True)  10.2 us
    all_to_all x1, blocking collectives, exchange(): lax.all_to_all(blocks, 'head', 0, 0, axis_index_groups=groups, tiled=True)  9.68 us
    all_gather x1, blocking collectives, finish(): sums = lax.all_gather(total, 'head', axis_index_groups=pairs)  7.78 us
    pallas_call x1, Pallas kernels, attend_and_pick(): pl.pallas_call(attend_kernel, out_shape=(jax.ShapeDtypeStruct((ROWS, FEW...  2.96 us
    pallas_call x1, Pallas kernels, normalize(): pl.pallas_call(functools.partial(norm_kernel, offsets), out_shape=(jax.Sh...  1.5 us
    all_to_all x2, waiting for transfers between devices, exchange(): lax.all_to_all(blocks, 'head', 0, 0, axis_index_groups=groups, tiled=True)  1.42 us
    pallas_call x1, Pallas kernels, project(): pl.pallas_call(project_kernel, out_shape=jax.ShapeDtypeStruct((CHIPS, 8,...  1.17 us
  transfers between devices with their start and end apart: 5, of which 2 were waited for; matrix products, arithmetic and copies ran while one was open for 0% of the time, Pallas kernels for 6%

profile of v6, /device:TPU:1, one launch (start us, length us, event | category | flops | bytes accessed | tf_op | source)
XLA Modules:
  0.0 46.9 jit_solution(4006154313908017385)
XLA Ops:
  0.6 0.0 copy-start
  0.6 0.0 copy-start.2
  0.7 0.0 copy-start.1
  0.7 0.0 copy-start.3
  0.7 3.0 %attend_and_pick.1 = (bf16[4,80,128]{2,1,0:T(8,128)(2,1)}, bf16[448,128]{1,0:T(8,128)(2,1)S(1)}, bf16[448,128]{1,0:T(8,128)(2,1)}, bf16[448,128]{1,0:T(8,128)(2,1)}, bf16[448,128]{1,0:T(8,128)(2,1)}) custom-call(s32[64]{0:T(128)} %slot_hbm.1, s32[4]{0:T(128)} %len_hbm.1, bf16[1,2,8,128,128]{4,3,2,1,0:T(8,128)(2,1)} %cache_ref.1, ...), custom_call_target="tpu_custom_call" | custom-call | bytes 12915000 | tf_op jit(solution)/shard_map/attend_and_pick/pallas_call | solution.py:150
  3.6 5.4 %all-to-all-start.2 = ((bf16[4,80,128]{2,1,0:T(8,128)(2,1)}), bf16[4,80,128]{2,1,0:T(8,128)(2,1)S(1)}, u32[]{:S(2)}, u32[]{:S(2)}) async-start(bf16[4,80,128]{2,1,0:T(8,128)(2,1)} %get-tuple-element.43), calls=%async_computation.2 | async-start | bytes 163840 | tf_op jit(solution)/shard_map/all_to_all | solution.py:372
  9.1 3.4 %collective-permute-start.2 = (bf16[448,128]{1,0:T(8,128)(2,1)}, bf16[448,128]{1,0:T(8,128)(2,1)S(1)}, u32[]{:S(2)}, u32[]{:S(2)}) collective-permute-start(bf16[448,128]{1,0:T(8,128)(2,1)} %get-tuple-element.42), channel_id=1, source_target_pairs={{0,8},{1,9},{2,10},{3,11},{4,12},{5,13},{6,14},{7,15},{8,16},{9,17... | collective-permute-start | bytes 344072 | tf_op jit(solution)/shard_map/ppermute | solution.py:385
  12.4 1.3 %all-to-all-done.2 = bf16[4,80,128]{2,1,0:T(8,128)(2,1)S(1)} async-done(((bf16[4,80,128]{2,1,0:T(8,128)(2,1)}), bf16[4,80,128]{2,1,0:T(8,128)(2,1)S(1)}, u32[]{:S(2)}, u32[]{:S(2)}) %all-to-all-start.2) | async-done | bytes 81952 | tf_op jit(solution)/shard_map/all_to_all | solution.py:372
  13.7 0.0 copy-done
  13.7 0.0 copy-done.2
  13.7 0.0 copy-done.1
  13.7 0.0 copy-done.3
  13.7 32.4 %conditional.2 = ((bf16[4,2,6144]{2,1,0:T(2,128)(2,1)}, bf16[4,2,192]{2,1,0:T(2,128)(2,1)}, bf16[1,4,512,128]{3,2,1,0:T(8,128)(2,1)})) conditional(s32[]{:T(128)} %convert_element_type.6, () %tuple.21, (bf16[4,80,128]{2,1,0:T(8,128)(2,1)S(1)}, bf16[256,6144]{1,0:T(8,128)(2,1)S(1)}, bf16[16,128]{1,0:T(8,128)(2,1)S(1)}, ...), branch_computations={%region_0.0_spmd, %region_1.0_spmd} | conditional | flops 4 | bytes 12885050 | solution.py:391
  13.7 1.2 %project.1 = bf16[16,8,384]{2,1,0:T(8,128)(2,1)} custom-call(bf16[4,80,128]{2,1,0:T(8,128)(2,1)S(1)} %get-tuple-element.22.att_ref.early_ref, bf16[256,6144]{1,0:T(8,128)(2,1)S(1)} %get-tuple-element.23.weight_ref, bf16[16,128]{1,0:T(8,128)(2,1)S(1)} %get-tuple-element.24.refs_0_), custom_call_target="tpu_custom_call" | custom-call | bytes 2214000 | tf_op jit(solution)/shard_map/cond/branch_1_fun/project/pallas_call | solution.py:205
  14.9 4.7 %all-to-all-start.1 = ((bf16[16,8,384]{2,1,0:T(8,128)(2,1)}), bf16[16,8,384]{2,1,0:T(8,128)(2,1)S(1)}, u32[]{:S(2)}, u32[]{:S(2)}) async-start(bf16[16,8,384]{2,1,0:T(8,128)(2,1)} %project.1), calls=%async_computation.1 | async-start | bytes 196608 | tf_op jit(solution)/shard_map/cond/branch_1_fun/all_to_all | solution.py:372
  19.6 4.2 %collective-permute-start = (bf16[448,128]{1,0:T(8,128)(2,1)}, bf16[448,128]{1,0:T(8,128)(2,1)S(1)}, u32[]{:S(2)}, u32[]{:S(2)}) collective-permute-start(bf16[448,128]{1,0:T(8,128)(2,1)} %get-tuple-element.29), channel_id=1, source_target_pairs={{0,16},{1,17},{2,18},{3,19},{4,20},{5,21},{6,22},{7,23},{8,24},{9,... | collective-permute-start | bytes 344072 | tf_op jit(solution)/shard_map/cond/branch_1_fun/ppermute | solution.py:385
  23.8 3.1 %collective-permute-start.1 = (bf16[448,128]{1,0:T(8,128)(2,1)}, bf16[448,128]{1,0:T(8,128)(2,1)S(1)}, u32[]{:S(2)}, u32[]{:S(2)}) collective-permute-start(bf16[448,128]{1,0:T(8,128)(2,1)} %get-tuple-element.30), channel_id=1, source_target_pairs={{0,24},{1,25},{2,26},{3,27},{4,28},{5,29},{6,30},{7,31},{8,0},{9,1... | collective-permute-start | bytes 344072 | tf_op jit(solution)/shard_map/cond/branch_1_fun/ppermute | solution.py:385
  26.9 0.1 widen.1.residual_ref
  27.0 0.2 all-to-all-done.1.parts_ref
  27.2 17.5 %conditional = (bf16[16,8,384]{2,1,0:T(8,128)(2,1)S(1)}) conditional(s32[]{:T(128)} %convert_element_type.4, () %tuple.16, f32[8,384]{1,0:T(8,128)S(1)} %add_residual.1), branch_computations={%region_2.0_spmd, %region_3.0_spmd} | conditional | bytes 971480 | solution.py:391
  27.2 7.8 %all-gather = f32[16,384]{1,0:T(8,128)S(1)} all-gather(f32[8,384]{1,0:T(8,128)S(1)} %param.2), channel_id=2, replica_groups={{0,1},{2,3},{4,5},{6,7},{8,9},{10,11},{12,13},{14,15},{16,17},{18,19},{..., dimensions={0}, use_global_device_ids=true | all-gather | bytes 36864 | tf_op jit(solution)/shard_map/cond/branch_1_fun/cond/branch_1_fun/all_gather | solution.py:394
  35.0 9.7 %all_to_all.13 = bf16[16,8,384]{2,1,0:T(8,128)(2,1)S(1)} all-to-all(bf16[16,8,384]{2,1,0:T(8,128)(2,1)S(1)} %round_hidden.1), channel_id=1, replica_groups={{4,12,20,28,6,14,22,30,0,8,16,24,2,10,18,26},{5,13,21,29,7,15,23,31,1,9..., dimensions={0} | all-to-all | bytes 196608 | tf_op jit(solution)/shard_map/cond/branch_1_fun/cond/branch_1_fun/all_to_all | solution.py:372
  44.7 0.0 collective-permute-done.refs_1_
  44.7 0.0 collective-permute-done.1.refs_2_
  44.7 1.5 %normalize.1 = (bf16[4,2,6144]{2,1,0:T(2,128)(2,1)}, bf16[4,2,192]{2,1,0:T(2,128)(2,1)}, bf16[1,4,512,128]{3,2,1,0:T(8,128)(2,1)}) custom-call(bf16[16,8,384]{2,1,0:T(8,128)(2,1)S(1)} %get-tuple-element.62.blocks_ref, f32[48,128]{1,0:T(8,128)S(1)} %bitcast.5, f32[48,128]{1,0:T(8,128)S(1)} %bitcast.6, ...), custom_call_target="tpu_custom_call" | custom-call | bytes 5166000 | tf_op jit(solution)/shard_map/cond/branch_1_fun/normalize/pallas_call | solution.py:330
  46.2 0.0 collective-permute-done.2.block_ref
  46.2 0.7 %place_last.1 = bf16[1,4,512,128]{3,2,1,0:T(8,128)(2,1)} custom-call(bf16[448,128]{1,0:T(8,128)(2,1)S(1)} %collective-permute-done.2.block_ref, bf16[1,4,512,128]{3,2,1,0:T(8,128)(2,1)} %get-tuple-element.47._), custom_call_target="tpu_custom_call", output_to_operand_aliasing={{}: (1, {})} | custom-call | bytes 2214000 | tf_op jit(solution)/shard_map/place_last/pallas_call | solution.py:358
  (3 shorter events, 0.0 us)
Async XLA Ops:
  0.6 13.1 %copy-start = (bf16[256,6144]{1,0:T(8,128)(2,1)S(1)}, bf16[256,6144]{1,0:T(8,128)(2,1)}, u32[]{:S(2)}) copy-start(bf16[256,6144]{1,0:T(8,128)(2,1)} %weight_ref.1) | copy-start | bytes 9437188
  0.6 13.1 %copy-start.2 = (f32[6144]{0:T(1024)S(1)}, f32[6144]{0:T(1024)}, u32[]{:S(2)}) copy-start(f32[6144]{0:T(1024)} %param.19) | copy-start | bytes 73732
  0.7 13.1 %copy-start.1 = (f32[6144]{0:T(1024)S(1)}, f32[6144]{0:T(1024)}, u32[]{:S(2)}) copy-start(f32[6144]{0:T(1024)} %param.18) | copy-start | bytes 73732
  0.7 13.1 %copy-start.3 = (bf16[4,2,192]{2,1,0:T(2,128)(2,1)S(1)}, bf16[4,2,192]{2,1,0:T(2,128)(2,1)}, u32[]{:S(2)}) copy-start(bf16[4,2,192]{2,1,0:T(2,128)(2,1)} %param.17) | copy-start | bytes 9220
  3.6 10.1 %all-to-all-start.2 = ((bf16[4,80,128]{2,1,0:T(8,128)(2,1)}), bf16[4,80,128]{2,1,0:T(8,128)(2,1)S(1)}, u32[]{:S(2)}, u32[]{:S(2)}) async-start(bf16[4,80,128]{2,1,0:T(8,128)(2,1)} %get-tuple-element.43), calls=%async_computation.2 | async-start | bytes 163840 | tf_op jit(solution)/shard_map/all_to_all | solution.py:372
  9.1 37.1 %collective-permute-start.2 = (bf16[448,128]{1,0:T(8,128)(2,1)}, bf16[448,128]{1,0:T(8,128)(2,1)S(1)}, u32[]{:S(2)}, u32[]{:S(2)}) collective-permute-start(bf16[448,128]{1,0:T(8,128)(2,1)} %get-tuple-element.42), channel_id=1, source_target_pairs={{0,8},{1,9},{2,10},{3,11},{4,12},{5,13},{6,14},{7,15},{8,16},{9,17... | collective-permute-start | bytes 344072 | tf_op jit(solution)/shard_map/ppermute | solution.py:385
  14.9 12.2 %all-to-all-start.1 = ((bf16[16,8,384]{2,1,0:T(8,128)(2,1)}), bf16[16,8,384]{2,1,0:T(8,128)(2,1)S(1)}, u32[]{:S(2)}, u32[]{:S(2)}) async-start(bf16[16,8,384]{2,1,0:T(8,128)(2,1)} %project.1), calls=%async_computation.1 | async-start | bytes 196608 | tf_op jit(solution)/shard_map/cond/branch_1_fun/all_to_all | solution.py:372
  19.6 25.0 %collective-permute-start = (bf16[448,128]{1,0:T(8,128)(2,1)}, bf16[448,128]{1,0:T(8,128)(2,1)S(1)}, u32[]{:S(2)}, u32[]{:S(2)}) collective-permute-start(bf16[448,128]{1,0:T(8,128)(2,1)} %get-tuple-element.29), channel_id=1, source_target_pairs={{0,16},{1,17},{2,18},{3,19},{4,20},{5,21},{6,22},{7,23},{8,24},{9,... | collective-permute-start | bytes 344072 | tf_op jit(solution)/shard_map/cond/branch_1_fun/ppermute | solution.py:385
  23.8 20.9 %collective-permute-start.1 = (bf16[448,128]{1,0:T(8,128)(2,1)}, bf16[448,128]{1,0:T(8,128)(2,1)S(1)}, u32[]{:S(2)}, u32[]{:S(2)}) collective-permute-start(bf16[448,128]{1,0:T(8,128)(2,1)} %get-tuple-element.30), channel_id=1, source_target_pairs={{0,24},{1,25},{2,26},{3,27},{4,28},{5,29},{6,30},{7,31},{8,0},{9,1... | collective-permute-start | bytes 344072 | tf_op jit(solution)/shard_map/cond/branch_1_fun/ppermute | solution.py:385

commit v7 on v6

--- a/solution.py
+++ b/solution.py
@@ -20,6 +20,8 @@
 OLD = MEMBERS // ROWS
 SHARE = OUT // MEMBERS
 CHUNK = OUT // CHIPS
+LINE_ORDER = [1, 2, 3, 0]
+LINE_RANK = [LINE_ORDER.index(row) for row in range(ROWS)]
 SUM_ORDER = [0, 1, 2, 3, 4, 5, 6, 7, 8, 9, 10, 11, 12, 13, 14, 15]
 ROW_ORDER = [2, 6, 10, 14, 3, 7, 11, 15, 0, 4, 8, 12, 1, 5, 9, 13]
 SUM_RANK = [SUM_ORDER.index(chip) for chip in range(CHIPS)]
@@ -139,9 +141,9 @@
         pair = [
             att_scr[slot_scr[(target * OLD + lane) * HEAD_DEV + i]] for i in range(HEAD_DEV)
         ]
-        att_ref[target, :FEW] = jnp.concatenate(pair, axis=0).astype(BF16)
+        att_ref[LINE_RANK[target], :FEW] = jnp.concatenate(pair, axis=0).astype(BF16)
         slot = slot_scr[(target * OLD + lane) * HEAD_DEV + HEAD_DEV - 1]
-        att_ref[target, FEW:] = held[1, slot, LEN - EARLY :]
+        att_ref[LINE_RANK[target], FEW:] = held[1, slot, LEN - EARLY :]
     for copy in copies:
         copy.wait()
 
@@ -290,7 +292,7 @@
     copies = place(offsets, kv_refs, cache_ref, sems)
     for row in range(ROWS):
         copy = pltpu.make_async_copy(
-            early_ref.at[row, pl.ds(FEW, EARLY)],
+            early_ref.at[LINE_RANK[row], pl.ds(FEW, EARLY)],
             cache_ref.at[0, row, pl.ds(LATE, EARLY)],
             sems.at[len(copies)],
         )
@@ -373,7 +375,7 @@
 
 
 def body(cache, fresh, slot_map, lengths, out_weight, residual, norm_gain, norm_bias):
-    columns = [[row * OLD + lane for row in range(ROWS)] for lane in range(OLD)]
+    columns = [[row * OLD + lane for row in LINE_ORDER] for lane in range(OLD)]
     sum_sides = [[chip * CORES + core for chip in SUM_ORDER] for core in range(CORES)]
     row_sides = [[chip * CORES + core for chip in ROW_ORDER] for core in range(CORES)]
     pairs = [[chip * CORES + core for core in range(CORES)] for chip in range(CHIPS)]

time: 47.3 us -> 46.1 us (0.975)
  blocking collectives: 17.5 us -> 16.3 us
    all_gather x1, blocking collectives: 7.78 us -> 6.15 us  [finish(): sums = lax.all_gather(total, 'head', axis_index_groups=pairs)]
    ppermute x3, starting transfers between devices: 10.6 us -> 9.16 us  [shifted(): return lax.ppermute(kv[offset], 'head', pairs)]
    all_to_all x2, starting transfers between devices: 10.2 us -> 11.3 us  [exchange(): lax.all_to_all(blocks, 'head', 0, 0, axis_index_groups=groups, tiled=True)]
    all_to_all x1, blocking collectives: 9.68 us -> 10.2 us  [exchange(): lax.all_to_all(blocks, 'head', 0, 0, axis_index_groups=groups, tiled=True)]
where the time goes in v7:
time: 46.1 us; the launch traced here: 45.7 us
  starting transfers between devices  20.5 us (44%)
  blocking collectives  16.3 us (35%)
  Pallas kernels  6.43 us (14%)
  waiting for transfers between devices  1.74 us (4%)
  between operations  0.72 us (2%)
    all_to_all x2, starting transfers between devices, exchange(): lax.all_to_all(blocks, 'head', 0, 0, axis_index_groups=groups, tiled=True)  11.3 us
    all_to_all x1, blocking collectives, exchange(): lax.all_to_all(blocks, 'head', 0, 0, axis_index_groups=groups, tiled=True)  10.2 us
    ppermute x3, starting transfers between devices, shifted(): return lax.ppermute(kv[offset], 'head', pairs)  9.16 us
    all_gather x1, blocking collectives, finish(): sums = lax.all_gather(total, 'head', axis_index_groups=pairs)  6.15 us
    pallas_call x1, Pallas kernels, attend_and_pick(): pl.pallas_call(attend_kernel, out_shape=(jax.ShapeDtypeStruct((ROWS, FEW...  2.96 us
    all_to_all x2, waiting for transfers between devices, exchange(): lax.all_to_all(blocks, 'head', 0, 0, axis_index_groups=groups, tiled=True)  1.74 us
    pallas_call x1, Pallas kernels, normalize(): pl.pallas_call(functools.partial(norm_kernel, offsets), out_shape=(jax.Sh...  1.5 us
    pallas_call x1, Pallas kernels, project(): pl.pallas_call(project_kernel, out_shape=jax.ShapeDtypeStruct((CHIPS, 8,...  1.17 us
  transfers between devices with their start and end apart: 5, of which 2 were waited for; matrix products, arithmetic and copies ran while one was open for 0% of the time, Pallas kernels for 6%

profile of v7, /device:TPU:1, one launch (start us, length us, event | category | flops | bytes accessed | tf_op | source)
XLA Modules:
  0.0 45.7 jit_solution(5298299223789319527)
XLA Ops:
  0.6 0.0 copy-start
  0.6 0.0 copy-start.2
  0.7 0.0 copy-start.1
  0.7 0.0 copy-start.3
  0.7 3.0 %attend_and_pick.1 = (bf16[4,80,128]{2,1,0:T(8,128)(2,1)}, bf16[448,128]{1,0:T(8,128)(2,1)S(1)}, bf16[448,128]{1,0:T(8,128)(2,1)}, bf16[448,128]{1,0:T(8,128)(2,1)}, bf16[448,128]{1,0:T(8,128)(2,1)}) custom-call(s32[64]{0:T(128)} %slot_hbm.1, s32[4]{0:T(128)} %len_hbm.1, bf16[1,2,8,128,128]{4,3,2,1,0:T(8,128)(2,1)} %cache_ref.1, ...), custom_call_target="tpu_custom_call" | custom-call | bytes 12915000 | tf_op jit(solution)/shard_map/attend_and_pick/pallas_call | solution.py:152
  3.6 5.7 %all-to-all-start.2 = ((bf16[4,80,128]{2,1,0:T(8,128)(2,1)}), bf16[4,80,128]{2,1,0:T(8,128)(2,1)S(1)}, u32[]{:S(2)}, u32[]{:S(2)}) async-start(bf16[4,80,128]{2,1,0:T(8,128)(2,1)} %get-tuple-element.43), calls=%async_computation.2 | async-start | bytes 163840 | tf_op jit(solution)/shard_map/all_to_all | solution.py:374
  9.4 1.9 %collective-permute-start.2 = (bf16[448,128]{1,0:T(8,128)(2,1)}, bf16[448,128]{1,0:T(8,128)(2,1)S(1)}, u32[]{:S(2)}, u32[]{:S(2)}) collective-permute-start(bf16[448,128]{1,0:T(8,128)(2,1)} %get-tuple-element.42), channel_id=1, source_target_pairs={{0,8},{1,9},{2,10},{3,11},{4,12},{5,13},{6,14},{7,15},{8,16},{9,17... | collective-permute-start | bytes 344072 | tf_op jit(solution)/shard_map/ppermute | solution.py:387
  11.3 1.5 %all-to-all-done.2 = bf16[4,80,128]{2,1,0:T(8,128)(2,1)S(1)} async-done(((bf16[4,80,128]{2,1,0:T(8,128)(2,1)}), bf16[4,80,128]{2,1,0:T(8,128)(2,1)S(1)}, u32[]{:S(2)}, u32[]{:S(2)}) %all-to-all-start.2) | async-done | bytes 81952 | tf_op jit(solution)/shard_map/all_to_all | solution.py:374
  12.8 0.0 copy-done
  12.8 0.0 copy-done.2
  12.8 0.0 copy-done.1
  12.8 0.0 copy-done.3
  12.8 32.2 %conditional.2 = ((bf16[4,2,6144]{2,1,0:T(2,128)(2,1)}, bf16[4,2,192]{2,1,0:T(2,128)(2,1)}, bf16[1,4,512,128]{3,2,1,0:T(8,128)(2,1)})) conditional(s32[]{:T(128)} %convert_element_type.6, () %tuple.21, (bf16[4,80,128]{2,1,0:T(8,128)(2,1)S(1)}, bf16[256,6144]{1,0:T(8,128)(2,1)S(1)}, bf16[16,128]{1,0:T(8,128)(2,1)S(1)}, ...), branch_computations={%region_0.0_spmd, %region_1.0_spmd} | conditional | flops 4 | bytes 12885050 | solution.py:393
  12.8 1.2 %project.1 = bf16[16,8,384]{2,1,0:T(8,128)(2,1)} custom-call(bf16[4,80,128]{2,1,0:T(8,128)(2,1)S(1)} %get-tuple-element.22.att_ref.early_ref, bf16[256,6144]{1,0:T(8,128)(2,1)S(1)} %get-tuple-element.23.weight_ref, bf16[16,128]{1,0:T(8,128)(2,1)S(1)} %get-tuple-element.24.refs_0_), custom_call_target="tpu_custom_call" | custom-call | bytes 2214000 | tf_op jit(solution)/shard_map/cond/branch_1_fun/project/pallas_call | solution.py:207
  14.0 5.6 %all-to-all-start.1 = ((bf16[16,8,384]{2,1,0:T(8,128)(2,1)}), bf16[16,8,384]{2,1,0:T(8,128)(2,1)S(1)}, u32[]{:S(2)}, u32[]{:S(2)}) async-start(bf16[16,8,384]{2,1,0:T(8,128)(2,1)} %project.1), calls=%async_computation.1 | async-start | bytes 196608 | tf_op jit(solution)/shard_map/cond/branch_1_fun/all_to_all | solution.py:374
  19.6 4.2 %collective-permute-start = (bf16[448,128]{1,0:T(8,128)(2,1)}, bf16[448,128]{1,0:T(8,128)(2,1)S(1)}, u32[]{:S(2)}, u32[]{:S(2)}) collective-permute-start(bf16[448,128]{1,0:T(8,128)(2,1)} %get-tuple-element.29), channel_id=1, source_target_pairs={{0,16},{1,17},{2,18},{3,19},{4,20},{5,21},{6,22},{7,23},{8,24},{9,... | collective-permute-start | bytes 344072 | tf_op jit(solution)/shard_map/cond/branch_1_fun/ppermute | solution.py:387
  23.8 3.1 %collective-permute-start.1 = (bf16[448,128]{1,0:T(8,128)(2,1)}, bf16[448,128]{1,0:T(8,128)(2,1)S(1)}, u32[]{:S(2)}, u32[]{:S(2)}) collective-permute-start(bf16[448,128]{1,0:T(8,128)(2,1)} %get-tuple-element.30), channel_id=1, source_target_pairs={{0,24},{1,25},{2,26},{3,27},{4,28},{5,29},{6,30},{7,31},{8,0},{9,1... | collective-permute-start | bytes 344072 | tf_op jit(solution)/shard_map/cond/branch_1_fun/ppermute | solution.py:387
  26.9 0.1 widen.1.residual_ref
  27.0 0.2 all-to-all-done.1.parts_ref
  27.2 16.3 %conditional = (bf16[16,8,384]{2,1,0:T(8,128)(2,1)S(1)}) conditional(s32[]{:T(128)} %convert_element_type.4, () %tuple.16, f32[8,384]{1,0:T(8,128)S(1)} %add_residual.1), branch_computations={%region_2.0_spmd, %region_3.0_spmd} | conditional | bytes 971480 | solution.py:393
  27.2 6.1 %all-gather = f32[16,384]{1,0:T(8,128)S(1)} all-gather(f32[8,384]{1,0:T(8,128)S(1)} %param.2), channel_id=2, replica_groups={{0,1},{2,3},{4,5},{6,7},{8,9},{10,11},{12,13},{14,15},{16,17},{18,19},{..., dimensions={0}, use_global_device_ids=true | all-gather | bytes 36864 | tf_op jit(solution)/shard_map/cond/branch_1_fun/cond/branch_1_fun/all_gather | solution.py:396
  33.4 10.2 %all_to_all.13 = bf16[16,8,384]{2,1,0:T(8,128)(2,1)S(1)} all-to-all(bf16[16,8,384]{2,1,0:T(8,128)(2,1)S(1)} %round_hidden.1), channel_id=1, replica_groups={{4,12,20,28,6,14,22,30,0,8,16,24,2,10,18,26},{5,13,21,29,7,15,23,31,1,9..., dimensions={0} | all-to-all | bytes 196608 | tf_op jit(solution)/shard_map/cond/branch_1_fun/cond/branch_1_fun/all_to_all | solution.py:374
  43.5 0.0 collective-permute-done.refs_1_
  43.5 0.0 collective-permute-done.1.refs_2_
  43.5 1.5 %normalize.1 = (bf16[4,2,6144]{2,1,0:T(2,128)(2,1)}, bf16[4,2,192]{2,1,0:T(2,128)(2,1)}, bf16[1,4,512,128]{3,2,1,0:T(8,128)(2,1)}) custom-call(bf16[16,8,384]{2,1,0:T(8,128)(2,1)S(1)} %get-tuple-element.62.blocks_ref, f32[48,128]{1,0:T(8,128)S(1)} %bitcast.5, f32[48,128]{1,0:T(8,128)S(1)} %bitcast.6, ...), custom_call_target="tpu_custom_call" | custom-call | bytes 5166000 | tf_op jit(solution)/shard_map/cond/branch_1_fun/normalize/pallas_call | solution.py:332
  45.0 0.0 collective-permute-done.2.block_ref
  45.1 0.7 %place_last.1 = bf16[1,4,512,128]{3,2,1,0:T(8,128)(2,1)} custom-call(bf16[448,128]{1,0:T(8,128)(2,1)S(1)} %collective-permute-done.2.block_ref, bf16[1,4,512,128]{3,2,1,0:T(8,128)(2,1)} %get-tuple-element.47._), custom_call_target="tpu_custom_call", output_to_operand_aliasing={{}: (1, {})} | custom-call | bytes 2214000 | tf_op jit(solution)/shard_map/place_last/pallas_call | solution.py:360
  (3 shorter events, 0.0 us)
Async XLA Ops:
  0.6 12.2 %copy-start = (bf16[256,6144]{1,0:T(8,128)(2,1)S(1)}, bf16[256,6144]{1,0:T(8,128)(2,1)}, u32[]{:S(2)}) copy-start(bf16[256,6144]{1,0:T(8,128)(2,1)} %weight_ref.1) | copy-start | bytes 9437188
  0.6 12.2 %copy-start.2 = (f32[6144]{0:T(1024)S(1)}, f32[6144]{0:T(1024)}, u32[]{:S(2)}) copy-start(f32[6144]{0:T(1024)} %param.19) | copy-start | bytes 73732
  0.7 12.2 %copy-start.1 = (f32[6144]{0:T(1024)S(1)}, f32[6144]{0:T(1024)}, u32[]{:S(2)}) copy-start(f32[6144]{0:T(1024)} %param.18) | copy-start | bytes 73732
  0.7 12.2 %copy-start.3 = (bf16[4,2,192]{2,1,0:T(2,128)(2,1)S(1)}, bf16[4,2,192]{2,1,0:T(2,128)(2,1)}, u32[]{:S(2)}) copy-start(bf16[4,2,192]{2,1,0:T(2,128)(2,1)} %param.17) | copy-start | bytes 9220
  3.6 9.2 %all-to-all-start.2 = ((bf16[4,80,128]{2,1,0:T(8,128)(2,1)}), bf16[4,80,128]{2,1,0:T(8,128)(2,1)S(1)}, u32[]{:S(2)}, u32[]{:S(2)}) async-start(bf16[4,80,128]{2,1,0:T(8,128)(2,1)} %get-tuple-element.43), calls=%async_computation.2 | async-start | bytes 163840 | tf_op jit(solution)/shard_map/all_to_all | solution.py:374
  9.4 35.7 %collective-permute-start.2 = (bf16[448,128]{1,0:T(8,128)(2,1)}, bf16[448,128]{1,0:T(8,128)(2,1)S(1)}, u32[]{:S(2)}, u32[]{:S(2)}) collective-permute-start(bf16[448,128]{1,0:T(8,128)(2,1)} %get-tuple-element.42), channel_id=1, source_target_pairs={{0,8},{1,9},{2,10},{3,11},{4,12},{5,13},{6,14},{7,15},{8,16},{9,17... | collective-permute-start | bytes 344072 | tf_op jit(solution)/shard_map/ppermute | solution.py:387
  14.0 13.2 %all-to-all-start.1 = ((bf16[16,8,384]{2,1,0:T(8,128)(2,1)}), bf16[16,8,384]{2,1,0:T(8,128)(2,1)S(1)}, u32[]{:S(2)}, u32[]{:S(2)}) async-start(bf16[16,8,384]{2,1,0:T(8,128)(2,1)} %project.1), calls=%async_computation.1 | async-start | bytes 196608 | tf_op jit(solution)/shard_map/cond/branch_1_fun/all_to_all | solution.py:374
  19.6 23.9 %collective-permute-start = (bf16[448,128]{1,0:T(8,128)(2,1)}, bf16[448,128]{1,0:T(8,128)(2,1)S(1)}, u32[]{:S(2)}, u32[]{:S(2)}) collective-permute-start(bf16[448,128]{1,0:T(8,128)(2,1)} %get-tuple-element.29), channel_id=1, source_target_pairs={{0,16},{1,17},{2,18},{3,19},{4,20},{5,21},{6,22},{7,23},{8,24},{9,... | collective-permute-start | bytes 344072 | tf_op jit(solution)/shard_map/cond/branch_1_fun/ppermute | solution.py:387
  23.8 19.8 %collective-permute-start.1 = (bf16[448,128]{1,0:T(8,128)(2,1)}, bf16[448,128]{1,0:T(8,128)(2,1)S(1)}, u32[]{:S(2)}, u32[]{:S(2)}) collective-permute-start(bf16[448,128]{1,0:T(8,128)(2,1)} %get-tuple-element.30), channel_id=1, source_target_pairs={{0,24},{1,25},{2,26},{3,27},{4,28},{5,29},{6,30},{7,31},{8,0},{9,1... | collective-permute-start | bytes 344072 | tf_op jit(solution)/shard_map/cond/branch_1_fun/ppermute | solution.py:387
